TPU v7x, 128 devices: a whole 4x4x4 slice. The times are simulated.
128 devices in a mesh: rep: 2 (over x_lo), row: 64 (over z, y, x_hi, core).
Axes of the slice: x: 4 (x_hi: 2, x_lo: 2; x = x_hi * 2 + x_lo), y: 4, z: 4, core: 2. Of those that a mesh axis runs over, the one named last changes fastest.
Arguments:
- features: bfloat16 [131072, 128], P(('row', 'rep')), may hold values from -6 to 6
- blocks: bfloat16 [64, 2, 64, 2, 256, 256], P('row', 'rep'), may hold values from 0 to 0.049804688
- codes: int32 [64, 2, 64, 2], P('row', 'rep'), may hold values from 0 to 31, as said below
- counts: int32 [64, 2, 64], P('row', 'rep'), may hold values from 0 to 2
- weight: bfloat16 [128, 256], replicated, may hold values from -0.5 to 0.5
- bias: float32 [256], replicated, may hold values from -3 to 3
Outputs:
- mixed: bfloat16 [131072, 256], P(('row', 'rep'))
Inputs may be any that keep to these rules, and one draw needn't show every extreme that they name: `codes`: each slot names row block and column block as rowblock * 4 + colblock; the slots of one device and section are distinct; slots at or past the section's count are unused.
All inputs are finite; a program needn't handle non-finite values.
Results may differ from a plain program's by a relative error of at most 0.014.
Values may be sent and summed in bfloat16 or wider, within the bound.
No kernel may reach another device: no remote copies, remote signals or barrier semaphores. Data moves between devices by JAX's collectives and lax.ppermute only.
A program may use at most 128 MiB of HBM per device.

v0:
```python
import jax
import jax.numpy as jnp
from jax import lax
from jax.sharding import PartitionSpec as P


def place_terms(picked, weights, chosen, living, running, col_blocks):
    slot_count = weights.shape[1]
    row_blocks = running.shape[0]
    product = jnp.einsum("gkuv,gkvf->gkuf", weights, picked, preferred_element_type=jnp.float32)
    active = jnp.arange(slot_count, dtype=jnp.int32)[None, :] < living[:, None]
    placing = (
        ((chosen // col_blocks)[..., None] == jnp.arange(row_blocks, dtype=jnp.int32))
        & active[..., None]
    ).astype(jnp.float32)
    return jnp.einsum("gkr,gkuf->ruf", placing, product)


def section_terms(tiles, weights, chosen, living, running):
    groups = weights.shape[0]
    block_size = weights.shape[2]
    channels = tiles.shape[-1]
    col_blocks = tiles.shape[1] // block_size
    divided = tiles.reshape(groups, col_blocks, block_size, channels)
    selector = ((chosen % col_blocks)[..., None] == jnp.arange(col_blocks, dtype=jnp.int32)).astype(
        jnp.bfloat16
    )
    picked = jnp.einsum(
        "gkc,gcbf->gkbf", selector, divided, preferred_element_type=jnp.float32
    ).astype(jnp.bfloat16)
    return place_terms(picked, weights, chosen, living, running, col_blocks)


def body(features, blocks, codes, counts, weight, bias):
    rep_count = lax.axis_size("rep")
    local_rows = features.shape[0]
    channels = features.shape[1]
    block_size = blocks.shape[-1]
    row_blocks = rep_count * local_rows // block_size
    weights_all = blocks.reshape(blocks.shape[2:])
    chosen_all = codes.reshape(codes.shape[2:])
    living_all = counts.reshape(counts.shape[2:])
    running = jnp.zeros((row_blocks, block_size, channels), jnp.float32)
    piece = lax.all_gather(features, "row", axis=0, tiled=True)
    width = piece.shape[0] // local_rows
    running = section_terms(
        piece.reshape(width, local_rows, channels), weights_all, chosen_all, living_all, running
    )
    shares = lax.psum_scatter(
        running.reshape(row_blocks * block_size, channels), "rep", scatter_dimension=0, tiled=True
    )
    hidden = jnp.dot(shares.astype(jnp.bfloat16), weight, preferred_element_type=jnp.float32) + bias
    return jnp.maximum(hidden, 0.0).astype(jnp.bfloat16)


def solution(mesh):
    placed = (
        P(("row", "rep"), None),
        P("row", "rep", None, None, None, None),
        P("row", "rep", None, None),
        P("row", "rep", None),
        P(),
        P(),
    )
    return jax.shard_map(
        body, mesh=mesh, in_specs=placed, out_specs=P(("row", "rep"), None), check_vma=False
    )
```

profile of v0, /device:TPU:1, one launch (start us, length us, event | category | flops | bytes accessed | tf_op | source)
XLA Modules:
  0.0 199.6 jit_solution(10008687755503941790)
XLA Ops:
  6.5 0.0 copy-start
  6.5 0.0 all-gather.2.cloned.1.call-start
  6.5 0.7 all-gather.2.cloned.1.call-update
  7.3 0.0 reduce-scatter.2.cloned.1.call-start
  7.3 0.7 and_select_fusion.1
  8.0 0.1 copy.8
  8.1 0.7 iota_compare_fusion.1
  8.8 110.5 %all-gather.2.cloned.1.call-done = bf16[65536,128]{1,0:T(8,128)(2,1)} async-done(((bf16[1024,128]{1,0:T(8,128)(2,1)}), bf16[65536,128]{1,0:T(8,128)(2,1)}) %all-gather.2.cloned.1.call-update) | async-done | bytes 16777232 | tf_op jit(solution)/shard_map/all_gather | solution.py:44
  119.3 20.2 %fusion.4 = bf16[64,2,256,128]{3,1,2,0:T(2,128)(2,1)S(1)} fusion(bf16[64,4,256,128]{3,2,1,0:T(8,128)(2,1)} %bitcast.44, s32[64,2]{1,0:T(8,128)S(1)} %copy.8), kind=kOutput, calls=%fused_computation.5 | convolution fusion | flops 33554944 | bytes 25166336 | tf_op jit(solution)/shard_map/gkc,gcbf->gkbf/dot_general | solution.py:28
  139.5 12.9 %fusion.2 = bf16[64,2,128,256]{3,2,1,0:T(8,128)(2,1)} fusion(bf16[1,1,64,2,256,256]{5,4,3,2,1,0:T(8,128)(2,1)} %param.7, bf16[64,2,256,128]{3,1,2,0:T(2,128)(2,1)S(1)} %fusion.4), kind=kOutput, calls=%fused_computation.2 | convolution fusion | flops 2147483648 | bytes 33554432 | tf_op jit(solution)/shard_map/gkuv,gkvf->gkuf/dot_general | solution.py:10
  152.4 12.0 %copy.13 = bf16[64,2,128,256]{2,0,1,3:T(8,128)(2,1)} copy(bf16[64,2,128,256]{3,2,1,0:T(8,128)(2,1)} %fusion.2) | data formatting | bytes 16777216 | tf_op jit(solution)/shard_map/gkuv,gkvf->gkuf/dot_general | solution.py:10
  164.4 0.0 copy-start.1
  164.4 4.6 %fusion.6 = f32[8,256,128]{2,0,1:T(8,128)S(1)} fusion(bf16[64,2,128,256]{2,0,1,3:T(8,128)(2,1)} %copy.13, s32[64,2]{0,1:T(2,128)S(1)} %get-tuple-element.5, pred[64,2]{0,1:T(4,128)(4,1)S(1)} %iota_compare_fusion.1), kind=kOutput, calls=%fused_computation.7 | convolution fusion | flops 67110912 | bytes 9437824 | tf_op jit(solution)/shard_map/gkr,gkuf->ruf/dot_general | solution.py:16
  169.1 1.2 copy.9
  170.2 0.0 reduce-scatter.2.cloned.1.call-update
  170.3 20.4 %reduce-scatter.2.cloned.1.call-done = f32[1024,128]{1,0:T(8,128)} async-done(((f32[2048,128]{1,0:T(8,128)}), f32[1024,128]{1,0:T(8,128)}) %reduce-scatter.2.cloned.1.call-update) | async-done | bytes 524304 | tf_op jit(solution)/shard_map/reduce_scatter | solution.py:49
  190.7 0.0 copy-done
  190.7 0.0 copy-done.1
  190.7 2.1 %fusion.10 = bf16[1024,256]{1,0:T(8,128)(2,1)} fusion(bf16[128,256]{1,0:T(8,128)(2,1)S(1)} %copy-done, f32[256]{0:T(256)S(1)} %copy-done.1, f32[1024,128]{1,0:T(8,128)} %reduce-scatter.2.cloned.1.call-done), kind=kOutput, calls=%fused_computation.10 | convolution fusion | flops 68026368 | bytes 1115136 | tf_op jit(solution)/shard_map/dot_general | solution.py:52
Async XLA Ops:
  6.5 184.1 %copy-start = (bf16[128,256]{1,0:T(8,128)(2,1)S(1)}, bf16[128,256]{1,0:T(8,128)(2,1)}, u32[]{:S(2)}) copy-start(bf16[128,256]{1,0:T(8,128)(2,1)} %param.10) | copy-start | bytes 196612
  6.5 112.7 %all-gather.2.cloned.1.call-start = ((), (), s32[]{:S(2)}) async-start(), calls=%async_computation.1 | async-start | bytes 17039360 | tf_op jit(solution)/shard_map/all_gather | solution.py:44
  7.3 183.4 %reduce-scatter.2.cloned.1.call-start = ((), (), s32[]{:S(2)}) async-start(), calls=%async_computation.2 | async-start | bytes 1572864 | tf_op jit(solution)/shard_map/reduce_scatter | solution.py:49
  164.4 26.3 %copy-start.1 = (f32[256]{0:T(256)S(1)}, f32[256]{0:T(256)}, u32[]{:S(2)}) copy-start(f32[256]{0:T(256)} %param.11) | copy-start | bytes 3076
Sparse Core Ops, SparseCore 0:
  10.6 108.6 all-gather.1
  170.4 20.2 reduce-scatter.1
where the time goes:
time: 200 us
  waiting for transfers between devices  132 us (66%)
  matrix products  39.9 us (20%)
  between operations  13.4 us (7%)
  local copies, waits for them, and re-layouts  13.3 us (7%)
    all_gather x1, waiting for transfers between devices, body(): piece = lax.all_gather(features, 'row', axis=0, tiled=True)  111 us
    reduce_scatter x1, waiting for transfers between devices, body(): lax.psum_scatter(running.reshape(row_blocks * block_size, channels), 'rep...  20.4 us
    dot_general x1, matrix products, section_terms(): jnp.einsum('gkc,gcbf->gkbf', selector, divided, preferred_element_type=jn...  20.2 us
    dot_general x1, matrix products, place_terms(): jnp.einsum('gkuv,gkvf->gkuf', weights, picked, preferred_element_type=jnp...  12.9 us
    dot_general x1, local copies, waits for them, and re-layouts, place_terms(): jnp.einsum('gkuv,gkvf->gkuf', weights, picked, preferred_element_type=jnp...  12 us
    dot_general x1, matrix products, place_terms(): return jnp.einsum('gkr,gkuf->ruf', placing, product)  4.64 us
  transfers between devices with their start and end apart: 2, of which 2 were waited for; matrix products, arithmetic and copies ran while one was open for 1% of the time, Pallas kernels for 0%

commit v1 on v0

v1 whole, which is shorter than its diff:
```python
import functools

import jax
import jax.numpy as jnp
import numpy as np
from jax import lax
from jax.experimental import pallas as pl
from jax.experimental.pallas import tpu as pltpu
from jax.sharding import PartitionSpec as P

DIMS = (4, 4, 2, 2)
SLOTS = 2

HOME = (0, 0, 0)
ROUNDS = (
    (("P1", (HOME,)), ("M1", (HOME,)), ("X", (HOME,)), ("P2", (HOME,)), ("M2", (HOME,))),
    (
        ("P1", ((0, 0, 3), (0, 0, 1))),
        ("M1", ((0, 1, 0), (0, 0, 1))),
        ("X", ((0, 0, 3), (0, 0, 1))),
        ("P2", ((1, 0, 0), (0, 1, 0))),
        ("M2", ((1, 0, 0), (0, 0, 1))),
    ),
    (
        ("P1", ((1, 0, 1), (0, 0, 2))),
        ("M1", ((0, 1, 3), (1, 1, 0))),
        ("X", ((0, 2, 0), (0, 1, 1))),
        ("P2", ((1, 3, 0), (1, 1, 0))),
        ("M2", ((0, 2, 0), (0, 1, 1))),
    ),
    (
        ("P2", ((0, 2, 3),)),
        ("X", ((0, 3, 2),)),
        ("M1", ((1, 0, 2),)),
        ("P1", ((1, 0, 2),)),
        ("M2", ((1, 2, 0),)),
        ("D1", ((1, 0, 2),)),
    ),
)
STEPS = {"P1": (0, 1), "M1": (0, -1), "D1": (0, 2), "P2": (1, 1), "M2": (1, -1)}


def row_of(place):
    return int(np.ravel_multi_index(place, DIMS))


def pairs_of(channel):
    pairs = []
    for place in np.ndindex(*DIMS):
        to = list(place)
        if channel == "X":
            to[2] = 1 - to[2]
        elif channel == "C":
            to[3] = 1 - to[3]
        else:
            axis, by = STEPS[channel]
            axis = (axis + place[2]) % 2
            to[axis] = (to[axis] + by) % DIMS[axis]
        pairs.append((row_of(place), row_of(to)))
    return pairs


def arrived(channel, unit):
    t, a, b = unit
    if channel == "X":
        return (1 - t, b, a)
    axis, by = STEPS[channel]
    return (t, (a - by) % 4, b) if axis == 0 else (t, a, (b - by) % 4)


def send(x, channel):
    return lax.ppermute(x, "row", pairs_of(channel))


def rows_of_units(units, row, core):
    t, a, b = (np.array(v, np.int32) for v in zip(*units))
    z, y, h = row // 16, row // 4 % 4, row // 2 % 2
    z = (z + jnp.where(h == 0, a, b)) % 4
    y = (y + jnp.where(h == 0, b, a)) % 4
    return ((z * 4 + y) * 2 + (h + t) % 2) * 2 + core


def pack_kernel(spots, block, row_ids, codes, counts, *refs):
    arrays, out, sems = refs[:-2], refs[-2], refs[-1]

    def each(act):
        for n, (which, at) in enumerate(spots):
            owner = row_ids[n]
            for k in range(SLOTS):

                @pl.when(k < counts[owner])
                def _():
                    start = pl.multiple_of(at + codes[owner * SLOTS + k] % 4 * block, block)
                    act(
                        pltpu.make_async_copy(
                            arrays[which].at[pl.ds(start, block)], out.at[n * SLOTS + k], sems.at[n * SLOTS + k]
                        )
                    )

    each(lambda copy: copy.start())
    each(lambda copy: copy.wait())


def pack(arrays, spots, row_ids, codes, counts, block):
    channels = arrays[0].shape[1]
    n = len(spots) * SLOTS
    return pl.pallas_call(
        functools.partial(pack_kernel, spots, block),
        out_shape=jax.ShapeDtypeStruct((n, block, channels), jnp.bfloat16),
        in_specs=[pl.BlockSpec(memory_space=pltpu.SMEM)] * 3 + [pl.BlockSpec(memory_space=pl.ANY)] * len(arrays),
        out_specs=pl.BlockSpec(memory_space=pl.ANY),
        scratch_shapes=[pltpu.SemaphoreType.DMA((n,))],
        cost_estimate=pl.CostEstimate(flops=0, bytes_accessed=n * block * channels * 4, transcendentals=0),
        name="pack",
    )(row_ids, codes, counts, *arrays)


def terms_kernel(spots, n_packed, n_arrays, first, last, base, row_ids, codes, counts, blocks, *refs):
    arrays, refs = refs[:n_arrays], refs[n_arrays:]
    if n_packed:
        packed, refs = refs[0], refs[1:]
    if not first:
        total_in, refs = refs[0], refs[1:]
    if last:
        kept, sent, refs = refs[0], refs[1], refs[2:]
        total, refs = refs[0], refs[1:]
    else:
        total, refs = refs[0], refs[1:]
    weights, picked, weight_sems, picked_sems = refs
    block = weights.shape[1]
    n_units = len(spots) + n_packed

    def source(n, k):
        owner = row_ids[n]
        if n < len(spots):
            which, at = spots[n]
            start = pl.multiple_of(at + codes[owner * SLOTS + k] % 4 * block, block)
            return arrays[which].at[pl.ds(start, block)]
        return packed.at[(n - len(spots)) * SLOTS + k]

    for n in range(n_units):
        owner = row_ids[n]
        for k in range(SLOTS):

            @pl.when(k < counts[owner])
            def _():
                task = n * SLOTS + k
                pltpu.make_async_copy(blocks.at[owner, k], weights.at[task], weight_sems.at[task]).start()
                pltpu.make_async_copy(source(n, k), picked.at[task], picked_sems.at[task]).start()

    total[...] = jnp.zeros_like(total) if first else total_in[...]

    def step(task, carry):
        owner = row_ids[task // SLOTS]

        @pl.when(task % SLOTS < counts[owner])
        def _():
            pltpu.make_async_copy(blocks.at[0, 0], weights.at[task], weight_sems.at[task]).wait()
            pltpu.make_async_copy(picked.at[task], picked.at[task], picked_sems.at[task]).wait()
            target = (codes[owner * SLOTS + task % SLOTS] // 4 + base[0]) % 8
            rows = pl.ds(pl.multiple_of(target * block, block), block)
            total[rows, :] += jnp.dot(weights[task], picked[task], preferred_element_type=jnp.float32)

        return carry

    lax.fori_loop(0, n_units * SLOTS, step, 0)
    if last:
        half = kept.shape[0]
        kept[...] = total[:half, :]
        sent[...] = total[half:, :].astype(sent.dtype)


def terms(arrays, spots, packed, row_ids, base, codes, counts, blocks, running, last):
    block = blocks.shape[-1]
    channels = (arrays[0] if arrays else packed).shape[-1]
    n_packed = 0 if packed is None else packed.shape[0] // SLOTS
    n = (len(spots) + n_packed) * SLOTS
    rows = 8 * block
    operands = [base, row_ids, codes, counts, blocks, *arrays]
    specs = [pl.BlockSpec(memory_space=pltpu.SMEM)] * 4 + [pl.BlockSpec(memory_space=pl.ANY)] * (1 + len(arrays))
    if packed is not None:
        operands.append(packed)
        specs.append(pl.BlockSpec(memory_space=pl.ANY))
    if running is not None:
        operands.append(running)
        specs.append(pl.BlockSpec(memory_space=pltpu.VMEM))
    whole = jax.ShapeDtypeStruct((rows, channels), jnp.float32)
    scratch = [
        pltpu.VMEM((n, block, block), jnp.bfloat16),
        pltpu.VMEM((n, block, channels), jnp.bfloat16),
        pltpu.SemaphoreType.DMA((n,)),
        pltpu.SemaphoreType.DMA((n,)),
    ]
    if last:
        shapes = (
            jax.ShapeDtypeStruct((rows // 2, channels), jnp.float32),
            jax.ShapeDtypeStruct((rows // 2, channels), jnp.bfloat16),
        )
        scratch.insert(0, pltpu.VMEM((rows, channels), jnp.float32))
    else:
        shapes = whole
    vmem = pl.BlockSpec(memory_space=pltpu.VMEM)
    return pl.pallas_call(
        functools.partial(terms_kernel, spots, n_packed, len(arrays), running is None, last),
        out_shape=shapes,
        in_specs=specs,
        out_specs=(vmem, vmem) if last else vmem,
        scratch_shapes=scratch,
        compiler_params=pltpu.CompilerParams(vmem_limit_bytes=16 * 2**20),
        cost_estimate=pl.CostEstimate(
            flops=2 * n * block * block * channels,
            bytes_accessed=n * (block * block + block * channels) * 2,
            transcendentals=0,
        ),
        name="terms",
    )(*operands)


def body(features, blocks, codes, counts, weight, bias):
    block = blocks.shape[-1]
    size = features.shape[0]
    row = lax.axis_index("row").astype(jnp.int32)
    core = row % 2
    base = (4 * lax.axis_index("rep").astype(jnp.int32)).reshape(1)
    blocks = blocks.reshape(blocks.shape[2:])
    table = jnp.concatenate([codes.reshape(-1), counts.reshape(-1)])
    other = send(table, "C")
    codes, counts = table[: codes.size], table[codes.size :]
    other_codes, other_counts = other[: codes.size], other[codes.size :]

    held = {HOME: (0, 0)}
    everything = [(features, (HOME,))]
    groups = []
    for number, moves in enumerate(ROUNDS):
        fresh = []
        for channel, units in moves:
            sources = {held[u][0] for u in units}
            if len(sources) == 1 and set(everything[min(sources)][1]) == set(units):
                x, units = everything[min(sources)]
            else:
                x = [everything[held[u][0]][0][held[u][1] * size : (held[u][1] + 1) * size] for u in units]
                x = x[0] if len(x) == 1 else jnp.concatenate(x)
            fresh.append((send(x, channel), tuple(arrived(channel, u) for u in units)))
        group = [everything[0]] if number == 0 else []
        for x, units in fresh:
            for at, u in enumerate(units):
                assert u not in held, u
                held[u] = (len(everything), at)
            everything.append((x, units))
            group.append((x, units))
        groups.append(group)

    running, packed, packed_rows = None, None, None
    for group in groups + [[]]:
        arrays = [x for x, _ in group]
        units = [u for _, us in group for u in us]
        spots = tuple((i, at * size) for i, (_, us) in enumerate(group) for at in range(len(us)))
        ids = [] if not units else [rows_of_units(units, row, core)]
        if packed is not None:
            ids.append(packed_rows)
        ids = ids[0] if len(ids) == 1 else jnp.concatenate(ids)
        following = None
        if units:
            following = send(
                pack(arrays, spots, rows_of_units(units, row, core), other_codes, other_counts, block), "C"
            )
            following_rows = rows_of_units(units, row, 1 - core)
        running = terms(
            arrays, spots, packed, ids, base, codes, counts, blocks, running, not units
        )
        if units:
            packed, packed_rows = following, following_rows
    kept, sent = running
    received = lax.ppermute(sent, "rep", [(0, 1), (1, 0)])
    shares = (kept + received.astype(jnp.float32)).astype(jnp.bfloat16)
    hidden = jnp.dot(shares, weight, preferred_element_type=jnp.float32) + bias
    return jnp.maximum(hidden, 0.0).astype(jnp.bfloat16)


def solution(mesh):
    placed = (
        P(("row", "rep"), None),
        P("row", "rep", None, None, None, None),
        P("row", "rep", None, None),
        P("row", "rep", None),
        P(),
        P(),
    )
    return jax.shard_map(
        body, mesh=mesh, in_specs=placed, out_specs=P(("row", "rep"), None), check_vma=False
    )
```

time: 200 us -> 281 us (1.41)
  the two profiles are of different devices: /device:TPU:1 before, /device:TPU:24 now
where the time goes in v1:
time: 281 us; the launch traced here: 278 us
  starting transfers between devices  125 us (44%)
  Pallas kernels  101 us (36%)
  waiting for transfers between devices  27.9 us (10%)
  local copies, waits for them, and re-layouts  17.8 us (6%)
  other arithmetic  4.36 us (2%)
    ppermute x26, starting transfers between devices, send(): return lax.ppermute(x, 'row', pairs_of(channel))  124 us
    pallas_call x5, Pallas kernels, terms(): pl.pallas_call(functools.partial(terms_kernel, spots, n_packed, len(array...  59.3 us
    pallas_call x4, Pallas kernels, pack(): pl.pallas_call(functools.partial(pack_kernel, spots, block), out_shape=ja...  41.8 us
    ppermute x26, waiting for transfers between devices, send(): return lax.ppermute(x, 'row', pairs_of(channel))  22.2 us
    unnamed x124, local copies, waits for them, and re-layouts  13.3 us
    ppermute x1, waiting for transfers between devices, body(): received = lax.ppermute(sent, 'rep', [(0, 1), (1, 0)])  5.72 us
  transfers between devices with their start and end apart: 27, of which 8 were waited for; matrix products, arithmetic and copies ran while one was open for 3% of the time, Pallas kernels for 34%

profile of v1, /device:TPU:24, one launch (start us, length us, event | category | flops | bytes accessed | tf_op | source)
XLA Modules:
  0.0 278.3 jit_solution(4141022980801745685)
XLA Ops:
  0.7 6.3 %collective-permute-start.1 = (bf16[1024,128]{1,0:T(8,128)(2,1)}, bf16[1024,128]{1,0:T(8,128)(2,1)S(1)}, u32[]{:S(2)}, u32[]{:S(2)}) collective-permute-start(bf16[1024,128]{1,0:T(8,128)(2,1)} %refs_0_.3), channel_id=1, source_target_pairs={{0,2},{1,3},{2,0},{3,1},{4,6},{5,7},{6,4},{7,5},{8,10},{9,11},{10,... | collective-permute-start | bytes 786440 | tf_op jit(solution)/shard_map/ppermute | solution.py:72
  7.7 1.8 collective-permute-done.5.refs_5_
  9.5 3.9 %collective-permute-done.1.refs_3_ = bf16[1024,128]{1,0:T(8,128)(2,1)S(1)} collective-permute-done((bf16[1024,128]{1,0:T(8,128)(2,1)}, bf16[1024,128]{1,0:T(8,128)(2,1)S(1)}, u32[]{:S(2)}, u32[]{:S(2)}) %collective-permute-start.1) | collective-permute-done | bytes 262176 | tf_op jit(solution)/shard_map/ppermute | solution.py:72
  13.3 1.4 collective-permute-done.2.refs_2_
  16.2 1.7 collective-permute-start.6
  17.8 3.2 %collective-permute-start.12 = (bf16[2048,128]{1,0:T(8,128)(2,1)S(1)}, bf16[2048,128]{1,0:T(8,128)(2,1)S(1)}, u32[]{:S(2)}, u32[]{:S(2)}) collective-permute-start(bf16[2048,128]{1,0:T(8,128)(2,1)S(1)} %get-tuple-element.19), channel_id=1, source_target_pairs={{0,48},{1,49},{2,14},{3,15},{4,52},{5,53},{6,2},{7,3},{8,56},{9,57... | collective-permute-start | bytes 1572872 | tf_op jit(solution)/shard_map/ppermute | solution.py:72
  21.8 6.1 %collective-permute-done.3.refs_3_ = bf16[2048,128]{1,0:T(8,128)(2,1)S(1)} collective-permute-done((bf16[2048,128]{1,0:T(8,128)(2,1)S(1)}, bf16[2048,128]{1,0:T(8,128)(2,1)S(1)}, u32[]{:S(2)}, u32[]{:S(2)}) %collective-permute-start.3) | collective-permute-done | bytes 524320 | tf_op jit(solution)/shard_map/ppermute | solution.py:72
  28.0 1.7 collective-permute-done.6.refs_2_
  30.6 2.0 collective-permute-start.7
  33.2 3.3 %collective-permute-start.13 = (bf16[2048,128]{1,0:T(8,128)(2,1)S(1)}, bf16[2048,128]{1,0:T(8,128)(2,1)S(1)}, u32[]{:S(2)}, u32[]{:S(2)}) collective-permute-start(bf16[2048,128]{1,0:T(8,128)(2,1)S(1)} %collective-permute-done.12.refs_1_), channel_id=1, source_target_pairs={{0,2},{1,3},{2,0},{3,1},{4,6},{5,7},{6,4},{7,5},{8,10},{9,11},{10,... | collective-permute-start | bytes 1572872 | tf_op jit(solution)/shard_map/ppermute | solution.py:72
  37.0 3.2 %collective-permute-start.19 = (bf16[2048,128]{1,0:T(8,128)(2,1)S(1)}, bf16[2048,128]{1,0:T(8,128)(2,1)}, u32[]{:S(2)}, u32[]{:S(2)}) collective-permute-start(bf16[2048,128]{1,0:T(8,128)(2,1)S(1)} %collective-permute-done.6.refs_2_), channel_id=1, source_target_pairs={{0,4},{1,5},{2,18},{3,19},{4,8},{5,9},{6,22},{7,23},{8,12},{9,13},... | collective-permute-start | bytes 1572872 | tf_op jit(solution)/shard_map/ppermute | solution.py:72
  40.3 1.6 collective-permute-done.7.refs_1_
  43.7 5.7 %collective-permute-done.22.refs_0_ = bf16[2048,128]{1,0:T(8,128)(2,1)S(1)} collective-permute-done((bf16[2048,128]{1,0:T(8,128)(2,1)}, bf16[2048,128]{1,0:T(8,128)(2,1)S(1)}, u32[]{:S(2)}, u32[]{:S(2)}) %collective-permute-start.22) | collective-permute-done | bytes 524320 | tf_op jit(solution)/shard_map/ppermute | solution.py:72
  53.1 12.0 %pack.6 = bf16[20,256,128]{2,1,0:T(8,128)(2,1)} custom-call(s32[10]{0:T(128)} %get-tuple-element.11.row_ids, s32[128]{0:T(128)} %slice.26.codes, s32[64]{0:T(128)} %slice.27.counts, bf16[2048,128]{1,0:T(8,128)(2,1)} %copy-done.25, bf16[2048,128]{1,0:T(8,128)(2,1)} %copy-done.21, bf16[2048,128]{1,0:T(8,128)(2,1)} %copy-done.9, bf16[2048,128]{1,0:T(8,128)(2,1)} %copy-done.7, ...), custom_call_target="tpu_custom_call" | custom-call | bytes 2621440 | tf_op jit(solution)/shard_map/pack/pallas_call | solution.py:107
  65.9 28.5 %collective-permute-start.23 = (bf16[20,256,128]{2,1,0:T(8,128)(2,1)}, bf16[20,256,128]{2,1,0:T(8,128)(2,1)}, u32[]{:S(2)}, u32[]{:S(2)}) collective-permute-start(bf16[20,256,128]{2,1,0:T(8,128)(2,1)} %pack.6), channel_id=1, source_target_pairs={{0,1},{1,0},{2,3},{3,2},{4,5},{5,4},{6,7},{7,6},{8,9},{9,8},{10,11... | collective-permute-start | bytes 3932168 | tf_op jit(solution)/shard_map/ppermute | solution.py:72
  94.4 4.0 %collective-permute-start.14 = (bf16[1024,128]{1,0:T(8,128)(2,1)}, bf16[1024,128]{1,0:T(8,128)(2,1)S(1)}, u32[]{:S(2)}, u32[]{:S(2)}) collective-permute-start(bf16[1024,128]{1,0:T(8,128)(2,1)} %slice.38), channel_id=1, source_target_pairs={{0,48},{1,49},{2,14},{3,15},{4,52},{5,53},{6,2},{7,3},{8,56},{9,57... | collective-permute-start | bytes 786440 | tf_op jit(solution)/shard_map/ppermute | solution.py:72
  99.0 17.9 %pack.5 = bf16[20,256,128]{2,1,0:T(8,128)(2,1)} custom-call(s32[10]{0:T(128)} %get-tuple-element.13.row_ids, s32[128]{0:T(128)} %slice.26.codes, s32[64]{0:T(128)} %slice.27.counts, bf16[2048,128]{1,0:T(8,128)(2,1)} %copy-done.13, bf16[2048,128]{1,0:T(8,128)(2,1)} %copy-done.3, bf16[2048,128]{1,0:T(8,128)(2,1)} %copy-done.11, ...), custom_call_target="tpu_custom_call" | custom-call | bytes 2621440 | tf_op jit(solution)/shard_map/pack/pallas_call | solution.py:107
  117.6 23.9 %collective-permute-start.21 = (bf16[20,256,128]{2,1,0:T(8,128)(2,1)}, bf16[20,256,128]{2,1,0:T(8,128)(2,1)S(1)}, u32[]{:S(2)}, u32[]{:S(2)}) collective-permute-start(bf16[20,256,128]{2,1,0:T(8,128)(2,1)} %pack.5), channel_id=1, source_target_pairs={{0,1},{1,0},{2,3},{3,2},{4,5},{5,4},{6,7},{7,6},{8,9},{9,8},{10,11... | collective-permute-start | bytes 3932168 | tf_op jit(solution)/shard_map/ppermute | solution.py:72
  141.5 1.7 slice.37
  144.1 3.0 %collective-permute-start.11 = (bf16[1024,128]{1,0:T(8,128)(2,1)}, bf16[1024,128]{1,0:T(8,128)(2,1)}, u32[]{:S(2)}, u32[]{:S(2)}) collective-permute-start(bf16[1024,128]{1,0:T(8,128)(2,1)} %slice.37), channel_id=1, source_target_pairs={{0,2},{1,3},{2,0},{3,1},{4,6},{5,7},{6,4},{7,5},{8,10},{9,11},{10,... | collective-permute-start | bytes 786440 | tf_op jit(solution)/shard_map/ppermute | solution.py:72
  147.1 4.0 %pack.7 = bf16[12,256,128]{2,1,0:T(8,128)(2,1)} custom-call(s32[6]{0:T(128)} %get-tuple-element.9.row_ids, s32[128]{0:T(128)} %slice.26.codes, s32[64]{0:T(128)} %slice.27.counts, bf16[1024,128]{1,0:T(8,128)(2,1)} %refs_0_.3, bf16[1024,128]{1,0:T(8,128)(2,1)} %copy-done.29, bf16[1024,128]{1,0:T(8,128)(2,1)} %copy-done.17, bf16[1024,128]{1,0:T(8,128)(2,1)} %copy-done.15, ...), custom_call_target="tpu_custom_call" | custom-call | bytes 1572864 | tf_op jit(solution)/shard_map/pack/pallas_call | solution.py:107
  151.2 21.7 %collective-permute-start.25 = (bf16[12,256,128]{2,1,0:T(8,128)(2,1)}, bf16[12,256,128]{2,1,0:T(8,128)(2,1)}, u32[]{:S(2)}, u32[]{:S(2)}) collective-permute-start(bf16[12,256,128]{2,1,0:T(8,128)(2,1)} %pack.7), channel_id=1, source_target_pairs={{0,1},{1,0},{2,3},{3,2},{4,5},{5,4},{6,7},{7,6},{8,9},{9,8},{10,11... | collective-permute-start | bytes 2359304 | tf_op jit(solution)/shard_map/ppermute | solution.py:72
  173.0 7.9 %pack.4 = bf16[12,256,128]{2,1,0:T(8,128)(2,1)} custom-call(s32[6]{0:T(128)} %get-tuple-element.15.row_ids, s32[128]{0:T(128)} %slice.26.codes, s32[64]{0:T(128)} %slice.27.counts, bf16[1024,128]{1,0:T(8,128)(2,1)} %copy-done.31, bf16[1024,128]{1,0:T(8,128)(2,1)} %collective-permute-done.11.refs_1_, bf16[1024,128]{1,0:T(8,128)(2,1)} %copy-done.33, ...), custom_call_target="tpu_custom_call" | custom-call | bytes 1572864 | tf_op jit(solution)/shard_map/pack/pallas_call | solution.py:107
  180.9 18.5 %collective-permute-start.18 = (bf16[12,256,128]{2,1,0:T(8,128)(2,1)}, bf16[12,256,128]{2,1,0:T(8,128)(2,1)}, u32[]{:S(2)}, u32[]{:S(2)}) collective-permute-start(bf16[12,256,128]{2,1,0:T(8,128)(2,1)} %pack.4), channel_id=1, source_target_pairs={{0,1},{1,0},{2,3},{3,2},{4,5},{5,4},{6,7},{7,6},{8,9},{9,8},{10,11... | collective-permute-start | bytes 2359304 | tf_op jit(solution)/shard_map/ppermute | solution.py:72
  199.6 5.8 %copy-done.1 = bf16[1,1,64,2,256,256]{5,4,3,2,1,0:T(8,128)(2,1)S(1)} copy-done((bf16[1,1,64,2,256,256]{5,4,3,2,1,0:T(8,128)(2,1)S(1)}, bf16[1,1,64,2,256,256]{5,4,3,2,1,0:T(8,128)(2,1)}, u32[]{:S(2)}) %copy-start.1) | copy-done | bytes 16777240
  205.4 6.4 %terms.5.refs_6_ = f32[2048,128]{1,0:T(8,128)S(1)} custom-call(s32[1]{0:T(128)} %bitcast.base, s32[6]{0:T(128)S(1)} %copy-done.38, s32[128]{0:T(128)S(1)} %reshape.14.codes, s32[64]{0:T(128)S(1)} %bitcast.14, bf16[64,2,256,256]{3,2,1,0:T(8,128)(2,1)S(1)} %bitcast.6, bf16[1024,128]{1,0:T(8,128)(2,1)S(1)} %copy-done.28, bf16[1024,128]{1,0:T(8,128)(2,1)S(1)} %copy-done.30, ...), custom_call_target="tpu_custom_call" | custom-call | flops 201326592 | bytes 2359296 | tf_op jit(solution)/shard_map/terms/pallas_call | solution.py:203
  211.9 5.8 %copy-done.2 = bf16[1,1,64,2,256,256]{5,4,3,2,1,0:T(8,128)(2,1)S(1)} copy-done((bf16[1,1,64,2,256,256]{5,4,3,2,1,0:T(8,128)(2,1)S(1)}, bf16[1,1,64,2,256,256]{5,4,3,2,1,0:T(8,128)(2,1)}, u32[]{:S(2)}) %copy-start.2) | copy-done | bytes 16777240
  217.6 15.0 %terms.6.refs_6_ = f32[2048,128]{1,0:T(8,128)S(1)} custom-call(s32[1]{0:T(128)} %bitcast.base, s32[16]{0:T(128)S(1)} %pad_add_fusion.3.row_ids, s32[128]{0:T(128)S(1)} %reshape.14.codes, s32[64]{0:T(128)S(1)} %bitcast.15, bf16[64,2,256,256]{3,2,1,0:T(8,128)(2,1)S(1)} %bitcast.7, bf16[2048,128]{1,0:T(8,128)(2,1)S(1)} %copy-done.26, ...), custom_call_target="tpu_custom_call" | custom-call | flops 536870912 | bytes 6291456 | tf_op jit(solution)/shard_map/terms/pallas_call | solution.py:203
  232.8 17.3 %terms.7.refs_7_ = f32[2048,128]{1,0:T(8,128)S(1)} custom-call(s32[1]{0:T(128)} %bitcast.base, s32[20]{0:T(128)S(1)} %pad_add_fusion.2.row_ids, s32[128]{0:T(128)S(1)} %reshape.14.codes, s32[64]{0:T(128)S(1)} %bitcast.16, bf16[64,2,256,256]{3,2,1,0:T(8,128)(2,1)S(1)} %bitcast.8, bf16[2048,128]{1,0:T(8,128)(2,1)S(1)} %copy-done.14, ...), custom_call_target="tpu_custom_call" | custom-call | flops 671088640 | bytes 7864320 | tf_op jit(solution)/shard_map/terms/pallas_call | solution.py:203
  250.2 15.3 %terms.8.refs_1_ = f32[2048,128]{1,0:T(8,128)S(1)} custom-call(s32[1]{0:T(128)} %bitcast.base, s32[16]{0:T(128)S(1)} %pad_add_fusion.1.row_ids, s32[128]{0:T(128)S(1)} %reshape.14.codes, s32[64]{0:T(128)S(1)} %bitcast.17, bf16[64,2,256,256]{3,2,1,0:T(8,128)(2,1)S(1)} %bitcast.11, bf16[1024,128]{1,0:T(8,128)(2,1)S(1)} %copy-done.32, ...), custom_call_target="tpu_custom_call" | custom-call | flops 536870912 | bytes 6291456 | tf_op jit(solution)/shard_map/terms/pallas_call | solution.py:203
  265.4 5.3 %terms.9 = (f32[1024,128]{1,0:T(8,128)S(1)}, bf16[1024,128]{1,0:T(8,128)(2,1)S(1)}) custom-call(s32[1]{0:T(128)} %bitcast.base, s32[6]{0:T(128)S(1)} %broadcast_add_fusion.7.row_ids, s32[128]{0:T(128)S(1)} %reshape.14.codes, s32[64]{0:T(128)S(1)} %bitcast.18, bf16[64,2,256,256]{3,2,1,0:T(8,128)(2,1)S(1)} %bitcast.12, ...), custom_call_target="tpu_custom_call" | custom-call | flops 201326592 | bytes 2359296 | tf_op jit(solution)/shard_map/terms/pallas_call | solution.py:203
  271.5 5.7 %collective-permute-done.26 = bf16[1024,128]{1,0:T(8,128)(2,1)S(1)} collective-permute-done((bf16[1024,128]{1,0:T(8,128)(2,1)S(1)}, bf16[1024,128]{1,0:T(8,128)(2,1)S(1)}, u32[]{:S(2)}, u32[]{:S(2)}) %collective-permute-start.26) | collective-permute-done | bytes 262176 | tf_op jit(solution)/shard_map/ppermute | solution.py:274
  (180 shorter events, 15.9 us)
Async XLA Ops:
  0.0 277.2 %copy-start = (bf16[128,256]{1,0:T(8,128)(2,1)S(1)}, bf16[128,256]{1,0:T(8,128)(2,1)}, u32[]{:S(2)}) copy-start(bf16[128,256]{1,0:T(8,128)(2,1)} %param.46) | copy-start | bytes 196612
  0.0 9.5 %collective-permute-start.5 = (bf16[1024,128]{1,0:T(8,128)(2,1)}, bf16[1024,128]{1,0:T(8,128)(2,1)S(1)}, u32[]{:S(2)}, u32[]{:S(2)}) collective-permute-start(bf16[1024,128]{1,0:T(8,128)(2,1)} %refs_0_.3), channel_id=1, source_target_pairs={{0,12},{1,13},{2,50},{3,51},{4,0},{5,1},{6,54},{7,55},{8,4},{9,5},... | collective-permute-start | bytes 786440 | tf_op jit(solution)/shard_map/ppermute | solution.py:72
  0.7 12.6 %collective-permute-start.1 = (bf16[1024,128]{1,0:T(8,128)(2,1)}, bf16[1024,128]{1,0:T(8,128)(2,1)S(1)}, u32[]{:S(2)}, u32[]{:S(2)}) collective-permute-start(bf16[1024,128]{1,0:T(8,128)(2,1)} %refs_0_.3), channel_id=1, source_target_pairs={{0,2},{1,3},{2,0},{3,1},{4,6},{5,7},{6,4},{7,5},{8,10},{9,11},{10,... | collective-permute-start | bytes 786440 | tf_op jit(solution)/shard_map/ppermute | solution.py:72
  7.1 7.7 %collective-permute-start.2 = (bf16[1024,128]{1,0:T(8,128)(2,1)}, bf16[1024,128]{1,0:T(8,128)(2,1)S(1)}, u32[]{:S(2)}, u32[]{:S(2)}) collective-permute-start(bf16[1024,128]{1,0:T(8,128)(2,1)} %refs_0_.3), channel_id=1, source_target_pairs={{0,48},{1,49},{2,14},{3,15},{4,52},{5,53},{6,2},{7,3},{8,56},{9,57... | collective-permute-start | bytes 786440 | tf_op jit(solution)/shard_map/ppermute | solution.py:72
  7.5 8.5 %collective-permute-start.4 = (bf16[1024,128]{1,0:T(8,128)(2,1)}, bf16[1024,128]{1,0:T(8,128)(2,1)S(1)}, u32[]{:S(2)}, u32[]{:S(2)}) collective-permute-start(bf16[1024,128]{1,0:T(8,128)(2,1)} %refs_0_.3), channel_id=1, source_target_pairs={{0,4},{1,5},{2,18},{3,19},{4,8},{5,9},{6,22},{7,23},{8,12},{9,13},... | collective-permute-start | bytes 786440 | tf_op jit(solution)/shard_map/ppermute | solution.py:72
  15.7 12.2 %collective-permute-start.3 = (bf16[2048,128]{1,0:T(8,128)(2,1)S(1)}, bf16[2048,128]{1,0:T(8,128)(2,1)S(1)}, u32[]{:S(2)}, u32[]{:S(2)}) collective-permute-start(bf16[2048,128]{1,0:T(8,128)(2,1)S(1)} %get-tuple-element.20), channel_id=1, source_target_pairs={{0,4},{1,5},{2,18},{3,19},{4,8},{5,9},{6,22},{7,23},{8,12},{9,13},... | collective-permute-start | bytes 1572872 | tf_op jit(solution)/shard_map/ppermute | solution.py:72
  16.2 13.5 %collective-permute-start.6 = (bf16[2048,128]{1,0:T(8,128)(2,1)S(1)}, bf16[2048,128]{1,0:T(8,128)(2,1)S(1)}, u32[]{:S(2)}, u32[]{:S(2)}) collective-permute-start(bf16[2048,128]{1,0:T(8,128)(2,1)S(1)} %constant_dynamic-update-slice_fusion), channel_id=1, source_target_pairs={{0,2},{1,3},{2,0},{3,1},{4,6},{5,7},{6,4},{7,5},{8,10},{9,11},{10,... | collective-permute-start | bytes 1572872 | tf_op jit(solution)/shard_map/ppermute | solution.py:72
  17.8 15.3 %collective-permute-start.12 = (bf16[2048,128]{1,0:T(8,128)(2,1)S(1)}, bf16[2048,128]{1,0:T(8,128)(2,1)S(1)}, u32[]{:S(2)}, u32[]{:S(2)}) collective-permute-start(bf16[2048,128]{1,0:T(8,128)(2,1)S(1)} %get-tuple-element.19), channel_id=1, source_target_pairs={{0,48},{1,49},{2,14},{3,15},{4,52},{5,53},{6,2},{7,3},{8,56},{9,57... | collective-permute-start | bytes 1572872 | tf_op jit(solution)/shard_map/ppermute | solution.py:72
  21.1 16.0 %collective-permute-start.9 = (bf16[2048,128]{1,0:T(8,128)(2,1)}, bf16[2048,128]{1,0:T(8,128)(2,1)S(1)}, u32[]{:S(2)}, u32[]{:S(2)}) collective-permute-start(bf16[2048,128]{1,0:T(8,128)(2,1)} %get-tuple-element.21), channel_id=1, source_target_pairs={{0,12},{1,13},{2,50},{3,51},{4,0},{5,1},{6,54},{7,55},{8,4},{9,5},... | collective-permute-start | bytes 1572872 | tf_op jit(solution)/shard_map/ppermute | solution.py:72
  30.6 11.3 %collective-permute-start.7 = (bf16[2048,128]{1,0:T(8,128)(2,1)}, bf16[2048,128]{1,0:T(8,128)(2,1)S(1)}, u32[]{:S(2)}, u32[]{:S(2)}) collective-permute-start(bf16[2048,128]{1,0:T(8,128)(2,1)} %pad_maximum_fusion.3), channel_id=1, source_target_pairs={{0,48},{1,49},{2,14},{3,15},{4,52},{5,53},{6,2},{7,3},{8,56},{9,57... | collective-permute-start | bytes 1572872 | tf_op jit(solution)/shard_map/ppermute | solution.py:72
  32.9 4.1 %collective-permute-start = (s32[192]{0:T(256)S(1)}, s32[192]{0:T(256)S(1)}, u32[]{:S(2)}, u32[]{:S(2)}) collective-permute-start(s32[192]{0:T(256)S(1)} %pad_add_fusion), channel_id=1, source_target_pairs={{0,1},{1,0},{2,3},{3,2},{4,5},{5,4},{6,7},{7,6},{8,9},{9,8},{10,11... | collective-permute-start | bytes 2312 | tf_op jit(solution)/shard_map/ppermute | solution.py:72
  33.1 16.2 %collective-permute-start.22 = (bf16[2048,128]{1,0:T(8,128)(2,1)}, bf16[2048,128]{1,0:T(8,128)(2,1)S(1)}, u32[]{:S(2)}, u32[]{:S(2)}) collective-permute-start(bf16[2048,128]{1,0:T(8,128)(2,1)} %copy-done.39), channel_id=1, source_target_pairs={{0,16},{1,17},{2,6},{3,7},{4,20},{5,21},{6,10},{7,11},{8,24},{9,25... | collective-permute-start | bytes 1572872 | tf_op jit(solution)/shard_map/ppermute | solution.py:72
  33.2 16.2 %collective-permute-start.13 = (bf16[2048,128]{1,0:T(8,128)(2,1)S(1)}, bf16[2048,128]{1,0:T(8,128)(2,1)S(1)}, u32[]{:S(2)}, u32[]{:S(2)}) collective-permute-start(bf16[2048,128]{1,0:T(8,128)(2,1)S(1)} %collective-permute-done.12.refs_1_), channel_id=1, source_target_pairs={{0,2},{1,3},{2,0},{3,1},{4,6},{5,7},{6,4},{7,5},{8,10},{9,11},{10,... | collective-permute-start | bytes 1572872 | tf_op jit(solution)/shard_map/ppermute | solution.py:72
  37.0 57.4 %collective-permute-start.20 = (bf16[2048,128]{1,0:T(8,128)(2,1)S(1)}, bf16[2048,128]{1,0:T(8,128)(2,1)}, u32[]{:S(2)}, u32[]{:S(2)}) collective-permute-start(bf16[2048,128]{1,0:T(8,128)(2,1)S(1)} %collective-permute-done.12.refs_1_), channel_id=1, source_target_pairs={{0,12},{1,13},{2,50},{3,51},{4,0},{5,1},{6,54},{7,55},{8,4},{9,5},... | collective-permute-start | bytes 1572872 | tf_op jit(solution)/shard_map/ppermute | solution.py:72
  37.0 57.4 %collective-permute-start.19 = (bf16[2048,128]{1,0:T(8,128)(2,1)S(1)}, bf16[2048,128]{1,0:T(8,128)(2,1)}, u32[]{:S(2)}, u32[]{:S(2)}) collective-permute-start(bf16[2048,128]{1,0:T(8,128)(2,1)S(1)} %collective-permute-done.6.refs_2_), channel_id=1, source_target_pairs={{0,4},{1,5},{2,18},{3,19},{4,8},{5,9},{6,22},{7,23},{8,12},{9,13},... | collective-permute-start | bytes 1572872 | tf_op jit(solution)/shard_map/ppermute | solution.py:72
  41.9 24.0 %collective-permute-start.10 = (bf16[2048,128]{1,0:T(8,128)(2,1)}, bf16[2048,128]{1,0:T(8,128)(2,1)S(1)}, u32[]{:S(2)}, u32[]{:S(2)}) collective-permute-start(bf16[2048,128]{1,0:T(8,128)(2,1)} %copy-done.23), channel_id=1, source_target_pairs={{0,16},{1,17},{2,6},{3,7},{4,20},{5,21},{6,10},{7,11},{8,24},{9,25... | collective-permute-start | bytes 1572872 | tf_op jit(solution)/shard_map/ppermute | solution.py:72
  49.3 67.6 %collective-permute-start.24 = (bf16[1024,128]{1,0:T(8,128)(2,1)S(1)}, bf16[1024,128]{1,0:T(8,128)(2,1)S(1)}, u32[]{:S(2)}, u32[]{:S(2)}) collective-permute-start(bf16[1024,128]{1,0:T(8,128)(2,1)S(1)} %copy-done.27), channel_id=1, source_target_pairs={{0,16},{1,17},{2,6},{3,7},{4,20},{5,21},{6,10},{7,11},{8,24},{9,25... | collective-permute-start | bytes 786440 | tf_op jit(solution)/shard_map/ppermute | solution.py:72
  50.2 67.5 %collective-permute-start.16 = (bf16[1024,128]{1,0:T(8,128)(2,1)}, bf16[1024,128]{1,0:T(8,128)(2,1)}, u32[]{:S(2)}, u32[]{:S(2)}) collective-permute-start(bf16[1024,128]{1,0:T(8,128)(2,1)} %get-tuple-element.17), channel_id=1, source_target_pairs={{0,12},{1,13},{2,50},{3,51},{4,0},{5,1},{6,54},{7,55},{8,4},{9,5},... | collective-permute-start | bytes 786440 | tf_op jit(solution)/shard_map/ppermute | solution.py:72
  65.9 166.8 %collective-permute-start.23 = (bf16[20,256,128]{2,1,0:T(8,128)(2,1)}, bf16[20,256,128]{2,1,0:T(8,128)(2,1)}, u32[]{:S(2)}, u32[]{:S(2)}) collective-permute-start(bf16[20,256,128]{2,1,0:T(8,128)(2,1)} %pack.6), channel_id=1, source_target_pairs={{0,1},{1,0},{2,3},{3,2},{4,5},{5,4},{6,7},{7,6},{8,9},{9,8},{10,11... | collective-permute-start | bytes 3932168 | tf_op jit(solution)/shard_map/ppermute | solution.py:72
  94.4 48.8 %collective-permute-start.8 = (bf16[1024,128]{1,0:T(8,128)(2,1)}, bf16[1024,128]{1,0:T(8,128)(2,1)S(1)}, u32[]{:S(2)}, u32[]{:S(2)}) collective-permute-start(bf16[1024,128]{1,0:T(8,128)(2,1)} %get-tuple-element.18), channel_id=1, source_target_pairs={{0,4},{1,5},{2,18},{3,19},{4,8},{5,9},{6,22},{7,23},{8,12},{9,13},... | collective-permute-start | bytes 786440 | tf_op jit(solution)/shard_map/ppermute | solution.py:72
  94.4 49.6 %collective-permute-start.14 = (bf16[1024,128]{1,0:T(8,128)(2,1)}, bf16[1024,128]{1,0:T(8,128)(2,1)S(1)}, u32[]{:S(2)}, u32[]{:S(2)}) collective-permute-start(bf16[1024,128]{1,0:T(8,128)(2,1)} %slice.38), channel_id=1, source_target_pairs={{0,48},{1,49},{2,14},{3,15},{4,52},{5,53},{6,2},{7,3},{8,56},{9,57... | collective-permute-start | bytes 786440 | tf_op jit(solution)/shard_map/ppermute | solution.py:72
  116.9 34.3 %collective-permute-start.15 = (bf16[1024,128]{1,0:T(8,128)(2,1)}, bf16[1024,128]{1,0:T(8,128)(2,1)S(1)}, u32[]{:S(2)}, u32[]{:S(2)}) collective-permute-start(bf16[1024,128]{1,0:T(8,128)(2,1)} %slice.38), channel_id=1, source_target_pairs={{0,16},{1,17},{2,6},{3,7},{4,20},{5,21},{6,10},{7,11},{8,24},{9,25... | collective-permute-start | bytes 786440 | tf_op jit(solution)/shard_map/ppermute | solution.py:72
  117.6 132.4 %collective-permute-start.21 = (bf16[20,256,128]{2,1,0:T(8,128)(2,1)}, bf16[20,256,128]{2,1,0:T(8,128)(2,1)S(1)}, u32[]{:S(2)}, u32[]{:S(2)}) collective-permute-start(bf16[20,256,128]{2,1,0:T(8,128)(2,1)} %pack.5), channel_id=1, source_target_pairs={{0,1},{1,0},{2,3},{3,2},{4,5},{5,4},{6,7},{7,6},{8,9},{9,8},{10,11... | collective-permute-start | bytes 3932168 | tf_op jit(solution)/shard_map/ppermute | solution.py:72
  143.2 29.8 %collective-permute-start.17 = (bf16[1024,128]{1,0:T(8,128)(2,1)}, bf16[1024,128]{1,0:T(8,128)(2,1)}, u32[]{:S(2)}, u32[]{:S(2)}) collective-permute-start(bf16[1024,128]{1,0:T(8,128)(2,1)} %slice.38), channel_id=1, source_target_pairs={{0,32},{1,33},{2,10},{3,11},{4,36},{5,37},{6,14},{7,15},{8,40},{9,... | collective-permute-start | bytes 786440 | tf_op jit(solution)/shard_map/ppermute | solution.py:72
  144.1 29.0 %collective-permute-start.11 = (bf16[1024,128]{1,0:T(8,128)(2,1)}, bf16[1024,128]{1,0:T(8,128)(2,1)}, u32[]{:S(2)}, u32[]{:S(2)}) collective-permute-start(bf16[1024,128]{1,0:T(8,128)(2,1)} %slice.37), channel_id=1, source_target_pairs={{0,2},{1,3},{2,0},{3,1},{4,6},{5,7},{6,4},{7,5},{8,10},{9,11},{10,... | collective-permute-start | bytes 786440 | tf_op jit(solution)/shard_map/ppermute | solution.py:72
  151.1 48.4 %copy-start.6 = (bf16[1024,128]{1,0:T(8,128)(2,1)S(1)}, bf16[1024,128]{1,0:T(8,128)(2,1)}, u32[]{:S(2)}) copy-start(bf16[1024,128]{1,0:T(8,128)(2,1)} %copy-done.5) | copy-start | bytes 786436
  151.1 48.4 %copy-start.16 = (bf16[1024,128]{1,0:T(8,128)(2,1)S(1)}, bf16[1024,128]{1,0:T(8,128)(2,1)}, u32[]{:S(2)}) copy-start(bf16[1024,128]{1,0:T(8,128)(2,1)} %copy-done.15) | copy-start | bytes 786436
  151.1 48.4 %copy-start.18 = (bf16[1024,128]{1,0:T(8,128)(2,1)S(1)}, bf16[1024,128]{1,0:T(8,128)(2,1)}, u32[]{:S(2)}) copy-start(bf16[1024,128]{1,0:T(8,128)(2,1)} %copy-done.17) | copy-start | bytes 786436
  151.2 48.4 %copy-start.20 = (bf16[1024,128]{1,0:T(8,128)(2,1)S(1)}, bf16[1024,128]{1,0:T(8,128)(2,1)}, u32[]{:S(2)}) copy-start(bf16[1024,128]{1,0:T(8,128)(2,1)} %copy-done.19) | copy-start | bytes 786436
  151.2 60.6 %collective-permute-start.25 = (bf16[12,256,128]{2,1,0:T(8,128)(2,1)}, bf16[12,256,128]{2,1,0:T(8,128)(2,1)}, u32[]{:S(2)}, u32[]{:S(2)}) collective-permute-start(bf16[12,256,128]{2,1,0:T(8,128)(2,1)} %pack.7), channel_id=1, source_target_pairs={{0,1},{1,0},{2,3},{3,2},{4,5},{5,4},{6,7},{7,6},{8,9},{9,8},{10,11... | collective-permute-start | bytes 2359304 | tf_op jit(solution)/shard_map/ppermute | solution.py:72
  180.9 84.5 %collective-permute-start.18 = (bf16[12,256,128]{2,1,0:T(8,128)(2,1)}, bf16[12,256,128]{2,1,0:T(8,128)(2,1)}, u32[]{:S(2)}, u32[]{:S(2)}) collective-permute-start(bf16[12,256,128]{2,1,0:T(8,128)(2,1)} %pack.4), channel_id=1, source_target_pairs={{0,1},{1,0},{2,3},{3,2},{4,5},{5,4},{6,7},{7,6},{8,9},{9,8},{10,11... | collective-permute-start | bytes 2359304 | tf_op jit(solution)/shard_map/ppermute | solution.py:72
  270.8 6.5 %collective-permute-start.26 = (bf16[1024,128]{1,0:T(8,128)(2,1)S(1)}, bf16[1024,128]{1,0:T(8,128)(2,1)S(1)}, u32[]{:S(2)}, u32[]{:S(2)}) collective-permute-start(bf16[1024,128]{1,0:T(8,128)(2,1)S(1)} %get-tuple-element.8), channel_id=1, source_target_pairs={{0,64},{64,0},{1,65},{65,1},{2,66},{66,2},{3,67},{67,3},{4,68},{68... | collective-permute-start | bytes 786440 | tf_op jit(solution)/shard_map/ppermute | solution.py:274
  (56 other events, 1143.9 us)

commit v2 on v1

v2 whole, which is shorter than its diff:
```python
import functools

import jax
import jax.numpy as jnp
import numpy as np
from jax import lax
from jax.experimental import pallas as pl
from jax.experimental.pallas import tpu as pltpu
from jax.sharding import PartitionSpec as P

DIMS = (4, 4, 2, 2)
SLOTS = 2
VMEM_LIMIT = 4 * 2**20
WIDTH = 2

HOME = (0, 0, 0)
ROUNDS = (
    (("P1", (HOME,)), ("M1", (HOME,)), ("X", (HOME,)), ("P2", (HOME,)), ("M2", (HOME,))),
    (
        ("P1", ((0, 0, 3), (0, 0, 1))),
        ("M1", ((0, 1, 0), (0, 0, 1))),
        ("X", ((0, 0, 3), (0, 0, 1))),
        ("P2", ((1, 0, 0), (0, 1, 0))),
        ("M2", ((1, 0, 0), (0, 0, 1))),
    ),
    (
        ("P1", ((1, 0, 1), (0, 0, 2))),
        ("M1", ((0, 1, 3), (1, 1, 0))),
        ("X", ((0, 2, 0), (0, 1, 1))),
        ("P2", ((1, 3, 0), (1, 1, 0))),
        ("M2", ((0, 2, 0), (0, 1, 1))),
    ),
    (
        ("D1", ((1, 0, 2),)),
        ("P1", ((1, 0, 2),)),
        ("X", ((0, 2, 1),)),
        ("P2", ((0, 2, 3), (1, 2, 0))),
        ("M2", ((1, 2, 0),)),
    ),
)
LATE = ("P2", "M2")
STEPS = {"P1": (0, 1), "M1": (0, -1), "D1": (0, 2), "P2": (1, 1), "M2": (1, -1)}


def row_of(place):
    return int(np.ravel_multi_index(place, DIMS))


def pairs_of(channel):
    pairs = []
    for place in np.ndindex(*DIMS):
        to = list(place)
        if channel == "X":
            to[2] = 1 - to[2]
        elif channel == "C":
            to[3] = 1 - to[3]
        else:
            axis, by = STEPS[channel]
            axis = (axis + place[2]) % 2
            to[axis] = (to[axis] + by * (1 - 2 * place[3])) % DIMS[axis]
        pairs.append((row_of(place), row_of(to)))
    return pairs


def arrived(channel, unit):
    t, a, b = unit
    if channel == "X":
        return (1 - t, b, a)
    axis, by = STEPS[channel]
    return (t, (a - by) % 4, b) if axis == 0 else (t, a, (b - by) % 4)


def send(x, channel):
    return lax.ppermute(x, "row", pairs_of(channel))


def owner_of(where, unit, core_flip):
    t, a, b = unit
    row = where[0]
    h = (row >> 1) & 1
    sign = 1 - 2 * ((row & 1) ^ core_flip)
    a, b = a * sign, b * sign
    z = ((row >> 4) + a + h * (b - a)) & 3
    y = (((row >> 2) & 3) + b + h * (a - b)) & 3
    return (((z * 4 + y) * 2 + (h ^ t)) << 1) + ((row & 1) ^ core_flip)


def pack_kernel(layout, block, where, codes, *refs):
    arrays, out = refs[:-1], refs[-1]
    n = 0
    for array, units in zip(arrays, layout):
        size = array.shape[0] // len(units)
        for at, unit in enumerate(units):
            owner = owner_of(where, unit, 0)
            for k in range(SLOTS):

                @pl.when(k < codes[SLOTS, owner])
                def _():
                    start = pl.multiple_of(at * size + (codes[k, owner] & 3) * block, block)
                    out[n * SLOTS + k] = array[pl.ds(start, block), :]

            n += 1


def pack(arrays, layout, where, codes, block):
    channels = arrays[0].shape[1]
    n = sum(map(len, layout)) * SLOTS
    vmem = pl.BlockSpec(memory_space=pltpu.VMEM)
    return pl.pallas_call(
        functools.partial(pack_kernel, layout, block),
        out_shape=jax.ShapeDtypeStruct((n, block, channels), jnp.bfloat16),
        in_specs=[pl.BlockSpec(memory_space=pltpu.SMEM)] * 2 + [vmem] * len(arrays),
        out_specs=vmem,
        cost_estimate=pl.CostEstimate(flops=0, bytes_accessed=n * block * channels * 4, transcendentals=0),
        compiler_params=pltpu.CompilerParams(vmem_limit_bytes=VMEM_LIMIT),
        name="pack",
    )(where, codes, *arrays)


def terms_kernel(layout, others, first, last, where, codes, blocks, *refs):
    arrays, refs = refs[: len(layout)], refs[len(layout) :]
    if others:
        packed, refs = refs[0], refs[1:]
    if not first:
        total_in, refs = refs[0], refs[1:]
    if last:
        kept, sent, refs = refs[0], refs[1], refs[2:]
    (total,) = refs
    block = blocks.shape[-1]
    units = [(u, 0) for us in layout for u in us] + [(u, 1) for u in others]

    total[...] = jnp.zeros_like(total) if first else total_in[...]
    base = where[1] * 4

    def products(pieces):
        found = []
        for owner, k, features in pieces:
            target = ((codes[k, owner] >> 2) + base) & 7
            rows = pl.ds(pl.multiple_of(target * block, block), block)
            found.append((rows, jnp.dot(blocks[owner, k], features, preferred_element_type=jnp.float32)))
        for rows, product in found:
            total[rows, :] += product

    def sweep(units, flip, features):
        for first in range(0, len(units), WIDTH):
            some = range(first, min(first + WIDTH, len(units)))
            owners = [owner_of(where, units[i], flip) for i in some]
            live = [codes[SLOTS, owner] for owner in owners]

            def pieces(which, slots, some=some, owners=owners):
                return [
                    (owners[n], k, features(some[n], codes[k, owners[n]], k))
                    for n in which
                    for k in range(slots)
                ]

            whole = functools.reduce(jnp.logical_and, [n == SLOTS for n in live])

            @pl.when(whole)
            def _():
                products(pieces(range(len(some)), SLOTS))

            @pl.when(jnp.logical_not(whole))
            def _():
                for n in range(len(some)):
                    for slots in range(1, SLOTS + 1):

                        @pl.when(live[n] == slots)
                        def _():
                            products(pieces([n], slots))

    for array, us in zip(arrays, layout):
        size = array.shape[0] // len(us)

        def features(i, code, k, array=array, size=size):
            return array[pl.ds(pl.multiple_of(i * size + (code & 3) * block, block), block), :]

        sweep(us, 0, features)
    if others:
        sweep(others, 1, lambda i, code, k: packed[i * SLOTS + k])
    if last:
        half = kept.shape[0]
        kept[...] = total[:half, :]
        sent[...] = total[half:, :].astype(sent.dtype)


def terms(arrays, layout, packed, others, where, codes, blocks, running, last):
    block = blocks.shape[-1]
    channels = (arrays[0] if arrays else packed).shape[-1]
    units = sum(map(len, layout)) + len(others)
    n = units * SLOTS
    rows = 8 * block
    vmem = pl.BlockSpec(memory_space=pltpu.VMEM)
    operands = [where, codes, blocks, *arrays]
    specs = [pl.BlockSpec(memory_space=pltpu.SMEM)] * 2 + [vmem] * (1 + len(arrays))
    for extra in (packed, running):
        if extra is not None:
            operands.append(extra)
            specs.append(vmem)
    scratch = []
    if last:
        shapes = (
            jax.ShapeDtypeStruct((rows // 2, channels), jnp.float32),
            jax.ShapeDtypeStruct((rows // 2, channels), jnp.bfloat16),
        )
        scratch.insert(0, pltpu.VMEM((rows, channels), jnp.float32))
    else:
        shapes = jax.ShapeDtypeStruct((rows, channels), jnp.float32)
    return pl.pallas_call(
        functools.partial(terms_kernel, layout, others, running is None, last),
        out_shape=shapes,
        in_specs=specs,
        out_specs=(vmem, vmem) if last else vmem,
        scratch_shapes=scratch,
        compiler_params=pltpu.CompilerParams(vmem_limit_bytes=VMEM_LIMIT),
        cost_estimate=pl.CostEstimate(
            flops=2 * n * block * block * channels,
            bytes_accessed=n * (block * block + block * channels) * 2,
            transcendentals=0,
        ),
        name="terms",
    )(*operands)


def load_kernel(source, out, sem):
    copy = pltpu.make_async_copy(source, out, sem)
    copy.start()
    copy.wait()


def load(blocks):
    return pl.pallas_call(
        load_kernel,
        out_shape=pltpu.VMEM(blocks.shape, blocks.dtype),
        in_specs=[pl.BlockSpec(memory_space=pltpu.HBM)],
        out_specs=pl.BlockSpec(memory_space=pltpu.VMEM),
        scratch_shapes=[pltpu.SemaphoreType.DMA(())],
        compiler_params=pltpu.CompilerParams(vmem_limit_bytes=VMEM_LIMIT),
        cost_estimate=pl.CostEstimate(flops=0, bytes_accessed=2 * blocks.size, transcendentals=0),
        name="load",
    )(pltpu.with_memory_space_constraint(blocks, pltpu.HBM))


def after(xs, *others):
    return list(lax.optimization_barrier((tuple(xs), others))[0])


def body(features, blocks, codes, counts, weight, bias):
    block = blocks.shape[-1]
    size = features.shape[0]
    where = jnp.stack([lax.axis_index("row"), lax.axis_index("rep")]).astype(jnp.int32)
    blocks = blocks.reshape(blocks.shape[2:])
    codes = jnp.concatenate([codes.reshape(codes.shape[2:]).T, counts.reshape(1, -1)])
    other_codes = send(codes, "C")

    held = {HOME: (0, 0)}
    everything = [(features, (HOME,))]
    group = everything[:]
    running, waiting = None, None

    def share(group):
        arrays, layout = [x for x, _ in group], tuple(us for _, us in group)
        packed = pack(arrays, layout, where, other_codes, block)
        return packed, tuple(u for us in layout for u in us)

    def add(group, packed, others, running, last=False):
        arrays, layout = [x for x, _ in group], tuple(us for _, us in group)
        return terms(arrays, layout, packed, others, where, codes, blocks, running, last)

    for number, moves in enumerate(ROUNDS):
        payloads = []
        for channel, units in moves:
            sources = {held[u][0] for u in units}
            if len(sources) == 1 and set(everything[min(sources)][1]) == set(units):
                x, units = everything[min(sources)]
            else:
                x = [everything[held[u][0]][0][held[u][1] * size : (held[u][1] + 1) * size] for u in units]
                x = x[0] if len(x) == 1 else jnp.concatenate(x)
            payloads.append((channel, x, units))
        if number:
            deps = [x for x, _ in group]
            if waiting is not None:
                running = add(*waiting, running)
                deps.append(running)
            else:
                blocks = load(blocks)
                deps.append(blocks)
            xs = after([x for x, _ in group], deps[-1])
            group = [(x, us) for x, (_, us) in zip(xs, group)]
            packed, others = share(group)
            deps.append(packed)
            packed = send(packed, "C")
            waiting = (group, packed, others)
            early = [p for p in payloads if p[0] not in LATE]
            late = [p for p in payloads if p[0] in LATE]
            xs = after([x for _, x, _ in early], *deps) + after([x for _, x, _ in late], *deps, packed)
            payloads = [(channel, x, units) for (channel, _, units), x in zip(early + late, xs)]
        group = group if number == 0 else []
        for channel, x, units in payloads:
            x, units = send(x, channel), tuple(arrived(channel, u) for u in units)
            for at, u in enumerate(units):
                assert u not in held, u
                held[u] = (len(everything), at)
            everything.append((x, units))
            group.append((x, units))
    assert len(held) == 32
    running = add(*waiting, running)
    xs = after([x for x, _ in group], running)
    group = [(x, us) for x, (_, us) in zip(xs, group)]
    packed, others = share(group)
    running = add(group, None, (), running)
    kept, sent = add([], send(packed, "C"), others, running, True)
    received = lax.ppermute(sent, "rep", [(0, 1), (1, 0)])
    shares = (kept + received.astype(jnp.float32)).astype(jnp.bfloat16)
    hidden = jnp.dot(shares, weight, preferred_element_type=jnp.float32) + bias
    return jnp.maximum(hidden, 0.0).astype(jnp.bfloat16)


def solution(mesh):
    placed = (
        P(("row", "rep"), None),
        P("row", "rep", None, None, None, None),
        P("row", "rep", None, None),
        P("row", "rep", None),
        P(),
        P(),
    )
    return jax.shard_map(
        body, mesh=mesh, in_specs=placed, out_specs=P(("row", "rep"), None), check_vma=False
    )
```

time: 281 us -> 93 us (0.33)
  the two profiles are of different devices: /device:TPU:24 before, /device:TPU:1 now
where the time goes in v2:
time: 93 us; the launch traced here: 93.5 us
  starting transfers between devices  39.6 us (43%)
  waiting for transfers between devices  27.3 us (29%)
  Pallas kernels  24.1 us (26%)
  matrix products  1.09 us (1%)
  other arithmetic  1.03 us (1%)
    ppermute x25, starting transfers between devices, send(): return lax.ppermute(x, 'row', pairs_of(channel))  38.4 us
    ppermute x25, waiting for transfers between devices, send(): return lax.ppermute(x, 'row', pairs_of(channel))  20.5 us
    pallas_call x5, Pallas kernels, terms(): pl.pallas_call(functools.partial(terms_kernel, layout, others, running is...  15 us
    ppermute x1, waiting for transfers between devices, body(): received = lax.ppermute(sent, 'rep', [(0, 1), (1, 0)])  6.8 us
    pallas_call x1, Pallas kernels, load(): pl.pallas_call(load_kernel, out_shape=pltpu.VMEM(blocks.shape, blocks.dty...  5.82 us
    pallas_call x4, Pallas kernels, pack(): pl.pallas_call(functools.partial(pack_kernel, layout, block), out_shape=j...  3.29 us
  transfers between devices with their start and end apart: 26, of which 13 were waited for; matrix products, arithmetic and copies ran while one was open for 1% of the time, Pallas kernels for 20%

profile of v2, /device:TPU:1, one launch (start us, length us, event | category | flops | bytes accessed | tf_op | source)
XLA Modules:
  0.0 93.5 jit_solution(4478953337924492950)
XLA Ops:
  0.0 3.6 %collective-permute-start.1 = (bf16[1024,128]{1,0:T(8,128)(2,1)}, bf16[1024,128]{1,0:T(8,128)(2,1)S(1)}, u32[]{:S(2)}, u32[]{:S(2)}) collective-permute-start(bf16[1024,128]{1,0:T(8,128)(2,1)} %refs_0_.1), channel_id=1, source_target_pairs={{0,2},{1,3},{2,0},{3,1},{4,6},{5,7},{6,4},{7,5},{8,10},{9,11},{10,... | collective-permute-start | bytes 786440 | tf_op jit(solution)/shard_map/ppermute | solution.py:74
  3.6 1.6 %collective-permute-start.2 = (bf16[1024,128]{1,0:T(8,128)(2,1)}, bf16[1024,128]{1,0:T(8,128)(2,1)S(1)}, u32[]{:S(2)}, u32[]{:S(2)}) collective-permute-start(bf16[1024,128]{1,0:T(8,128)(2,1)} %refs_0_.1), channel_id=1, source_target_pairs={{0,48},{1,17},{2,14},{3,7},{4,52},{5,21},{6,2},{7,11},{8,56},{9,25... | collective-permute-start | bytes 786440 | tf_op jit(solution)/shard_map/ppermute | solution.py:74
  5.2 1.3 %collective-permute-start.3 = (bf16[1024,128]{1,0:T(8,128)(2,1)}, bf16[1024,128]{1,0:T(8,128)(2,1)S(1)}, u32[]{:S(2)}, u32[]{:S(2)}) collective-permute-start(bf16[1024,128]{1,0:T(8,128)(2,1)} %refs_0_.1), channel_id=1, source_target_pairs={{0,12},{1,5},{2,50},{3,19},{4,0},{5,9},{6,54},{7,23},{8,4},{9,13},... | collective-permute-start | bytes 786440 | tf_op jit(solution)/shard_map/ppermute | solution.py:74
  6.5 1.4 %collective-permute-start.5 = (bf16[1024,128]{1,0:T(8,128)(2,1)}, bf16[1024,128]{1,0:T(8,128)(2,1)S(1)}, u32[]{:S(2)}, u32[]{:S(2)}) collective-permute-start(bf16[1024,128]{1,0:T(8,128)(2,1)} %refs_0_.1), channel_id=1, source_target_pairs={{0,4},{1,13},{2,18},{3,51},{4,8},{5,1},{6,22},{7,55},{8,12},{9,5},... | collective-permute-start | bytes 786440 | tf_op jit(solution)/shard_map/ppermute | solution.py:74
  8.0 2.1 %collective-permute-start.4 = (bf16[1024,128]{1,0:T(8,128)(2,1)}, bf16[1024,128]{1,0:T(8,128)(2,1)S(1)}, u32[]{:S(2)}, u32[]{:S(2)}) collective-permute-start(bf16[1024,128]{1,0:T(8,128)(2,1)} %refs_0_.1), channel_id=1, source_target_pairs={{0,16},{1,49},{2,6},{3,15},{4,20},{5,53},{6,10},{7,3},{8,24},{9,57... | collective-permute-start | bytes 786440 | tf_op jit(solution)/shard_map/ppermute | solution.py:74
  10.8 1.6 %collective-permute-start = (s32[3,64]{1,0:T(4,128)S(1)}, s32[3,64]{1,0:T(4,128)S(1)}, u32[]{:S(2)}, u32[]{:S(2)}) collective-permute-start(s32[3,64]{1,0:T(4,128)S(1)} %pad_add_fusion.codes), channel_id=1, source_target_pairs={{0,1},{1,0},{2,3},{3,2},{4,5},{5,4},{6,7},{7,6},{8,9},{9,8},{10,11... | collective-permute-start | bytes 2312 | tf_op jit(solution)/shard_map/ppermute | solution.py:74
  12.5 5.8 %load.1.blocks = bf16[64,2,256,256]{3,2,1,0:T(8,128)(2,1)S(1)} custom-call(bf16[64,2,256,256]{3,2,1,0:T(8,128)(2,1)} %bitcast.8), custom_call_target="tpu_custom_call" | custom-call | bytes 16777216 | tf_op jit(solution)/shard_map/load/pallas_call | solution.py:232
  20.6 2.7 %collective-permute-start.11 = (bf16[2048,128]{1,0:T(8,128)(2,1)S(1)}, bf16[2048,128]{1,0:T(8,128)(2,1)S(1)}, u32[]{:S(2)}, u32[]{:S(2)}) collective-permute-start(bf16[2048,128]{1,0:T(8,128)(2,1)S(1)} %get-tuple-element.53), channel_id=1, source_target_pairs={{0,16},{1,49},{2,6},{3,15},{4,20},{5,53},{6,10},{7,3},{8,24},{9,57... | collective-permute-start | bytes 1572872 | tf_op jit(solution)/shard_map/ppermute | solution.py:74
  24.0 2.7 %collective-permute-start.8 = (bf16[2048,128]{1,0:T(8,128)(2,1)S(1)}, bf16[2048,128]{1,0:T(8,128)(2,1)S(1)}, u32[]{:S(2)}, u32[]{:S(2)}) collective-permute-start(bf16[2048,128]{1,0:T(8,128)(2,1)S(1)} %get-tuple-element.50), channel_id=1, source_target_pairs={{0,4},{1,13},{2,18},{3,51},{4,8},{5,1},{6,22},{7,55},{8,12},{9,5},... | collective-permute-start | bytes 1572872 | tf_op jit(solution)/shard_map/ppermute | solution.py:74
  26.7 2.8 %terms.5.refs_6_ = f32[2048,128]{1,0:T(8,128)S(1)} custom-call(s32[2]{0:T(128)S(1)} %pad_add_fusion.1.where, s32[3,64]{1,0:T(4,128)S(1)} %pad_add_fusion.codes, bf16[64,2,256,256]{3,2,1,0:T(8,128)(2,1)S(1)} %load.1.blocks, bf16[1024,128]{1,0:T(8,128)(2,1)S(1)} %copy-done.1, bf16[1024,128]{1,0:T(8,128)(2,1)S(1)} %collective-permute-done.4.refs_1_, ...), custom_call_target="tpu_custom_call" | custom-call | flops 402653184 | bytes 4718592 | tf_op jit(solution)/shard_map/terms/pallas_call | solution.py:209
  29.4 3.1 %collective-permute-done.10.refs_1_ = bf16[2048,128]{1,0:T(8,128)(2,1)S(1)} collective-permute-done((bf16[2048,128]{1,0:T(8,128)(2,1)S(1)}, bf16[2048,128]{1,0:T(8,128)(2,1)S(1)}, u32[]{:S(2)}, u32[]{:S(2)}) %collective-permute-start.10) | collective-permute-done | bytes 524320 | tf_op jit(solution)/shard_map/ppermute | solution.py:74
  32.5 2.3 %collective-permute-done.11.refs_0_ = bf16[2048,128]{1,0:T(8,128)(2,1)S(1)} collective-permute-done((bf16[2048,128]{1,0:T(8,128)(2,1)S(1)}, bf16[2048,128]{1,0:T(8,128)(2,1)S(1)}, u32[]{:S(2)}, u32[]{:S(2)}) %collective-permute-start.11) | collective-permute-done | bytes 524320 | tf_op jit(solution)/shard_map/ppermute | solution.py:74
  34.8 3.5 %collective-permute-done.9.refs_2_ = bf16[2048,128]{1,0:T(8,128)(2,1)S(1)} collective-permute-done((bf16[2048,128]{1,0:T(8,128)(2,1)S(1)}, bf16[2048,128]{1,0:T(8,128)(2,1)S(1)}, u32[]{:S(2)}, u32[]{:S(2)}) %collective-permute-start.9) | collective-permute-done | bytes 524320 | tf_op jit(solution)/shard_map/ppermute | solution.py:74
  39.2 1.3 %collective-permute-start.13 = (bf16[20,256,128]{2,1,0:T(8,128)(2,1)S(1)}, bf16[20,256,128]{2,1,0:T(8,128)(2,1)S(1)}, u32[]{:S(2)}, u32[]{:S(2)}) collective-permute-start(bf16[20,256,128]{2,1,0:T(8,128)(2,1)S(1)} %pack.5), channel_id=1, source_target_pairs={{0,1},{1,0},{2,3},{3,2},{4,5},{5,4},{6,7},{7,6},{8,9},{9,8},{10,11... | collective-permute-start | bytes 3932168 | tf_op jit(solution)/shard_map/ppermute | solution.py:74
  40.7 2.3 %collective-permute-start.12 = (bf16[2048,128]{1,0:T(8,128)(2,1)S(1)}, bf16[2048,128]{1,0:T(8,128)(2,1)S(1)}, u32[]{:S(2)}, u32[]{:S(2)}) collective-permute-start(bf16[2048,128]{1,0:T(8,128)(2,1)S(1)} %collective-permute-done.10.refs_1_), channel_id=1, source_target_pairs={{0,2},{1,3},{2,0},{3,1},{4,6},{5,7},{6,4},{7,5},{8,10},{9,11},{10,... | collective-permute-start | bytes 1572872 | tf_op jit(solution)/shard_map/ppermute | solution.py:74
  42.9 2.8 %collective-permute-start.15 = (bf16[2048,128]{1,0:T(8,128)(2,1)S(1)}, bf16[2048,128]{1,0:T(8,128)(2,1)S(1)}, u32[]{:S(2)}, u32[]{:S(2)}) collective-permute-start(bf16[2048,128]{1,0:T(8,128)(2,1)S(1)} %collective-permute-done.7.refs_4_), channel_id=1, source_target_pairs={{0,16},{1,49},{2,6},{3,15},{4,20},{5,53},{6,10},{7,3},{8,24},{9,57... | collective-permute-start | bytes 1572872 | tf_op jit(solution)/shard_map/ppermute | solution.py:74
  46.0 2.6 %collective-permute-start.17 = (bf16[2048,128]{1,0:T(8,128)(2,1)S(1)}, bf16[2048,128]{1,0:T(8,128)(2,1)S(1)}, u32[]{:S(2)}, u32[]{:S(2)}) collective-permute-start(bf16[2048,128]{1,0:T(8,128)(2,1)S(1)} %collective-permute-done.9.refs_2_), channel_id=1, source_target_pairs={{0,4},{1,13},{2,18},{3,51},{4,8},{5,1},{6,22},{7,55},{8,12},{9,5},... | collective-permute-start | bytes 1572872 | tf_op jit(solution)/shard_map/ppermute | solution.py:74
  48.6 4.8 %terms.6.refs_6_ = f32[2048,128]{1,0:T(8,128)S(1)} custom-call(s32[2]{0:T(128)S(1)} %pad_add_fusion.1.where, s32[3,64]{1,0:T(4,128)S(1)} %pad_add_fusion.codes, bf16[64,2,256,256]{3,2,1,0:T(8,128)(2,1)S(1)} %load.1.blocks, bf16[2048,128]{1,0:T(8,128)(2,1)S(1)} %collective-permute-done.11.refs_0_, bf16[2048,128]{1,0:T(8,128)(2,1)S(1)} %collective-permute-done.10.refs_1_, ...), custom_call_target="tpu_custom_call" | custom-call | flops 671088640 | bytes 7864320 | tf_op jit(solution)/shard_map/terms/pallas_call | solution.py:209
  53.4 2.4 %collective-permute-done.12.refs_2_ = bf16[2048,128]{1,0:T(8,128)(2,1)S(1)} collective-permute-done((bf16[2048,128]{1,0:T(8,128)(2,1)S(1)}, bf16[2048,128]{1,0:T(8,128)(2,1)S(1)}, u32[]{:S(2)}, u32[]{:S(2)}) %collective-permute-start.12) | collective-permute-done | bytes 524320 | tf_op jit(solution)/shard_map/ppermute | solution.py:74
  56.5 2.3 %collective-permute-done.16.refs_1_ = bf16[2048,128]{1,0:T(8,128)(2,1)S(1)} collective-permute-done((bf16[2048,128]{1,0:T(8,128)(2,1)S(1)}, bf16[2048,128]{1,0:T(8,128)(2,1)S(1)}, u32[]{:S(2)}, u32[]{:S(2)}) %collective-permute-start.16) | collective-permute-done | bytes 524320 | tf_op jit(solution)/shard_map/ppermute | solution.py:74
  59.9 2.5 %collective-permute-start.21 = (bf16[20,256,128]{2,1,0:T(8,128)(2,1)S(1)}, bf16[20,256,128]{2,1,0:T(8,128)(2,1)S(1)}, u32[]{:S(2)}, u32[]{:S(2)}) collective-permute-start(bf16[20,256,128]{2,1,0:T(8,128)(2,1)S(1)} %pack.6), channel_id=1, source_target_pairs={{0,1},{1,0},{2,3},{3,2},{4,5},{5,4},{6,7},{7,6},{8,9},{9,8},{10,11... | collective-permute-start | bytes 3932168 | tf_op jit(solution)/shard_map/ppermute | solution.py:74
  62.4 2.6 %collective-permute-done.21.refs_5_ = bf16[20,256,128]{2,1,0:T(8,128)(2,1)S(1)} collective-permute-done((bf16[20,256,128]{2,1,0:T(8,128)(2,1)S(1)}, bf16[20,256,128]{2,1,0:T(8,128)(2,1)S(1)}, u32[]{:S(2)}, u32[]{:S(2)}) %collective-permute-start.21) | collective-permute-done | bytes 1310752 | tf_op jit(solution)/shard_map/ppermute | solution.py:74
  65.1 2.7 %collective-permute-start.22 = (bf16[2048,128]{1,0:T(8,128)(2,1)S(1)}, bf16[2048,128]{1,0:T(8,128)(2,1)S(1)}, u32[]{:S(2)}, u32[]{:S(2)}) collective-permute-start(bf16[2048,128]{1,0:T(8,128)(2,1)S(1)} %collective-permute-done.16.refs_1_), channel_id=1, source_target_pairs={{0,4},{1,13},{2,18},{3,51},{4,8},{5,1},{6,22},{7,55},{8,12},{9,5},... | collective-permute-start | bytes 1572872 | tf_op jit(solution)/shard_map/ppermute | solution.py:74
  67.8 1.2 %collective-permute-start.18 = (bf16[1024,128]{1,0:T(8,128)(2,1)S(1)}, bf16[1024,128]{1,0:T(8,128)(2,1)S(1)}, u32[]{:S(2)}, u32[]{:S(2)}) collective-permute-start(bf16[1024,128]{1,0:T(8,128)(2,1)S(1)} %slice.23), channel_id=1, source_target_pairs={{0,32},{1,33},{2,10},{3,11},{4,36},{5,37},{6,14},{7,15},{8,40},{9,... | collective-permute-start | bytes 786440 | tf_op jit(solution)/shard_map/ppermute | solution.py:74
  69.0 1.6 %collective-permute-start.19 = (bf16[1024,128]{1,0:T(8,128)(2,1)S(1)}, bf16[1024,128]{1,0:T(8,128)(2,1)S(1)}, u32[]{:S(2)}, u32[]{:S(2)}) collective-permute-start(bf16[1024,128]{1,0:T(8,128)(2,1)S(1)} %slice.23), channel_id=1, source_target_pairs={{0,16},{1,49},{2,6},{3,15},{4,20},{5,53},{6,10},{7,3},{8,24},{9,57... | collective-permute-start | bytes 786440 | tf_op jit(solution)/shard_map/ppermute | solution.py:74
  70.6 1.6 %collective-permute-start.20 = (bf16[1024,128]{1,0:T(8,128)(2,1)S(1)}, bf16[1024,128]{1,0:T(8,128)(2,1)S(1)}, u32[]{:S(2)}, u32[]{:S(2)}) collective-permute-start(bf16[1024,128]{1,0:T(8,128)(2,1)S(1)} %slice.24), channel_id=1, source_target_pairs={{0,2},{1,3},{2,0},{3,1},{4,6},{5,7},{6,4},{7,5},{8,10},{9,11},{10,... | collective-permute-start | bytes 786440 | tf_op jit(solution)/shard_map/ppermute | solution.py:74
  72.7 4.0 %terms.7.refs_5_ = f32[2048,128]{1,0:T(8,128)S(1)} custom-call(s32[2]{0:T(128)S(1)} %pad_add_fusion.1.where, s32[3,64]{1,0:T(4,128)S(1)} %pad_add_fusion.codes, bf16[64,2,256,256]{3,2,1,0:T(8,128)(2,1)S(1)} %load.1.blocks, bf16[2048,128]{1,0:T(8,128)(2,1)S(1)} %collective-permute-done.15.refs_0_, bf16[2048,128]{1,0:T(8,128)(2,1)S(1)} %collective-permute-done.16.refs_1_, ...), custom_call_target="tpu_custom_call" | custom-call | flops 671088640 | bytes 7864320 | tf_op jit(solution)/shard_map/terms/pallas_call | solution.py:209
  76.6 1.2 %collective-permute-done.18.refs_0_ = bf16[1024,128]{1,0:T(8,128)(2,1)S(1)} collective-permute-done((bf16[1024,128]{1,0:T(8,128)(2,1)S(1)}, bf16[1024,128]{1,0:T(8,128)(2,1)S(1)}, u32[]{:S(2)}, u32[]{:S(2)}) %collective-permute-start.18) | collective-permute-done | bytes 262176 | tf_op jit(solution)/shard_map/ppermute | solution.py:74
  77.9 1.2 %collective-permute-done.19.refs_1_ = bf16[1024,128]{1,0:T(8,128)(2,1)S(1)} collective-permute-done((bf16[1024,128]{1,0:T(8,128)(2,1)S(1)}, bf16[1024,128]{1,0:T(8,128)(2,1)S(1)}, u32[]{:S(2)}, u32[]{:S(2)}) %collective-permute-start.19) | collective-permute-done | bytes 262176 | tf_op jit(solution)/shard_map/ppermute | solution.py:74
  80.4 1.7 %terms.8.refs_1_ = f32[2048,128]{1,0:T(8,128)S(1)} custom-call(s32[2]{0:T(128)S(1)} %pad_add_fusion.1.where, s32[3,64]{1,0:T(4,128)S(1)} %pad_add_fusion.codes, bf16[64,2,256,256]{3,2,1,0:T(8,128)(2,1)S(1)} %load.1.blocks, bf16[1024,128]{1,0:T(8,128)(2,1)S(1)} %collective-permute-done.18.refs_0_, bf16[1024,128]{1,0:T(8,128)(2,1)S(1)} %collective-permute-done.19.refs_1_, ...), custom_call_target="tpu_custom_call" | custom-call | flops 201326592 | bytes 2359296 | tf_op jit(solution)/shard_map/terms/pallas_call | solution.py:209
  82.6 1.8 %terms.9 = (f32[1024,128]{1,0:T(8,128)S(1)}, bf16[1024,128]{1,0:T(8,128)(2,1)S(1)}) custom-call(s32[2]{0:T(128)S(1)} %pad_add_fusion.1.where, s32[3,64]{1,0:T(4,128)S(1)} %pad_add_fusion.codes, bf16[64,2,256,256]{3,2,1,0:T(8,128)(2,1)S(1)} %load.1.blocks, bf16[12,256,128]{2,1,0:T(8,128)(2,1)S(1)} %collective-permute-done.24.refs_0_, ...), custom_call_target="tpu_custom_call" | custom-call | flops 201326592 | bytes 2359296 | tf_op jit(solution)/shard_map/terms/pallas_call | solution.py:209
  85.6 6.8 %collective-permute-done.25 = bf16[1024,128]{1,0:T(8,128)(2,1)S(1)} collective-permute-done((bf16[1024,128]{1,0:T(8,128)(2,1)S(1)}, bf16[1024,128]{1,0:T(8,128)(2,1)S(1)}, u32[]{:S(2)}, u32[]{:S(2)}) %collective-permute-start.25) | collective-permute-done | bytes 262176 | tf_op jit(solution)/shard_map/ppermute | solution.py:313
  (46 shorter events, 11.4 us)
Async XLA Ops:
  0.0 92.4 %copy-start = (bf16[128,256]{1,0:T(8,128)(2,1)S(1)}, bf16[128,256]{1,0:T(8,128)(2,1)}, u32[]{:S(2)}) copy-start(bf16[128,256]{1,0:T(8,128)(2,1)} %param.10) | copy-start | bytes 196612
  0.0 10.8 %collective-permute-start.1 = (bf16[1024,128]{1,0:T(8,128)(2,1)}, bf16[1024,128]{1,0:T(8,128)(2,1)S(1)}, u32[]{:S(2)}, u32[]{:S(2)}) collective-permute-start(bf16[1024,128]{1,0:T(8,128)(2,1)} %refs_0_.1), channel_id=1, source_target_pairs={{0,2},{1,3},{2,0},{3,1},{4,6},{5,7},{6,4},{7,5},{8,10},{9,11},{10,... | collective-permute-start | bytes 786440 | tf_op jit(solution)/shard_map/ppermute | solution.py:74
  3.6 14.7 %collective-permute-start.2 = (bf16[1024,128]{1,0:T(8,128)(2,1)}, bf16[1024,128]{1,0:T(8,128)(2,1)S(1)}, u32[]{:S(2)}, u32[]{:S(2)}) collective-permute-start(bf16[1024,128]{1,0:T(8,128)(2,1)} %refs_0_.1), channel_id=1, source_target_pairs={{0,48},{1,17},{2,14},{3,7},{4,52},{5,21},{6,2},{7,11},{8,56},{9,25... | collective-permute-start | bytes 786440 | tf_op jit(solution)/shard_map/ppermute | solution.py:74
  5.2 13.1 %collective-permute-start.3 = (bf16[1024,128]{1,0:T(8,128)(2,1)}, bf16[1024,128]{1,0:T(8,128)(2,1)S(1)}, u32[]{:S(2)}, u32[]{:S(2)}) collective-permute-start(bf16[1024,128]{1,0:T(8,128)(2,1)} %refs_0_.1), channel_id=1, source_target_pairs={{0,12},{1,5},{2,50},{3,19},{4,0},{5,9},{6,54},{7,23},{8,4},{9,13},... | collective-permute-start | bytes 786440 | tf_op jit(solution)/shard_map/ppermute | solution.py:74
  6.5 11.8 %collective-permute-start.5 = (bf16[1024,128]{1,0:T(8,128)(2,1)}, bf16[1024,128]{1,0:T(8,128)(2,1)S(1)}, u32[]{:S(2)}, u32[]{:S(2)}) collective-permute-start(bf16[1024,128]{1,0:T(8,128)(2,1)} %refs_0_.1), channel_id=1, source_target_pairs={{0,4},{1,13},{2,18},{3,51},{4,8},{5,1},{6,22},{7,55},{8,12},{9,5},... | collective-permute-start | bytes 786440 | tf_op jit(solution)/shard_map/ppermute | solution.py:74
  8.0 10.4 %collective-permute-start.4 = (bf16[1024,128]{1,0:T(8,128)(2,1)}, bf16[1024,128]{1,0:T(8,128)(2,1)S(1)}, u32[]{:S(2)}, u32[]{:S(2)}) collective-permute-start(bf16[1024,128]{1,0:T(8,128)(2,1)} %refs_0_.1), channel_id=1, source_target_pairs={{0,16},{1,49},{2,6},{3,15},{4,20},{5,53},{6,10},{7,3},{8,24},{9,57... | collective-permute-start | bytes 786440 | tf_op jit(solution)/shard_map/ppermute | solution.py:74
  10.8 7.5 %collective-permute-start = (s32[3,64]{1,0:T(4,128)S(1)}, s32[3,64]{1,0:T(4,128)S(1)}, u32[]{:S(2)}, u32[]{:S(2)}) collective-permute-start(s32[3,64]{1,0:T(4,128)S(1)} %pad_add_fusion.codes), channel_id=1, source_target_pairs={{0,1},{1,0},{2,3},{3,2},{4,5},{5,4},{6,7},{7,6},{8,9},{9,8},{10,11... | collective-permute-start | bytes 2312 | tf_op jit(solution)/shard_map/ppermute | solution.py:74
  12.5 5.9 %copy-start.1 = (bf16[1024,128]{1,0:T(8,128)(2,1)S(1)}, bf16[1024,128]{1,0:T(8,128)(2,1)}, u32[]{:S(2)}) copy-start(bf16[1024,128]{1,0:T(8,128)(2,1)} %refs_0_.1) | copy-start | bytes 786436
  19.1 4.9 %collective-permute-start.6 = (bf16[12,256,128]{2,1,0:T(8,128)(2,1)S(1)}, bf16[12,256,128]{2,1,0:T(8,128)(2,1)S(1)}, u32[]{:S(2)}, u32[]{:S(2)}) collective-permute-start(bf16[12,256,128]{2,1,0:T(8,128)(2,1)S(1)} %pack.4), channel_id=1, source_target_pairs={{0,1},{1,0},{2,3},{3,2},{4,5},{5,4},{6,7},{7,6},{8,9},{9,8},{10,11... | collective-permute-start | bytes 2359304 | tf_op jit(solution)/shard_map/ppermute | solution.py:74
  20.5 12.0 %collective-permute-start.10 = (bf16[2048,128]{1,0:T(8,128)(2,1)S(1)}, bf16[2048,128]{1,0:T(8,128)(2,1)S(1)}, u32[]{:S(2)}, u32[]{:S(2)}) collective-permute-start(bf16[2048,128]{1,0:T(8,128)(2,1)S(1)} %get-tuple-element.52), channel_id=1, source_target_pairs={{0,48},{1,17},{2,14},{3,7},{4,52},{5,21},{6,2},{7,11},{8,56},{9,25... | collective-permute-start | bytes 1572872 | tf_op jit(solution)/shard_map/ppermute | solution.py:74
  20.6 14.2 %collective-permute-start.11 = (bf16[2048,128]{1,0:T(8,128)(2,1)S(1)}, bf16[2048,128]{1,0:T(8,128)(2,1)S(1)}, u32[]{:S(2)}, u32[]{:S(2)}) collective-permute-start(bf16[2048,128]{1,0:T(8,128)(2,1)S(1)} %get-tuple-element.53), channel_id=1, source_target_pairs={{0,16},{1,49},{2,6},{3,15},{4,20},{5,53},{6,10},{7,3},{8,24},{9,57... | collective-permute-start | bytes 1572872 | tf_op jit(solution)/shard_map/ppermute | solution.py:74
  23.2 15.1 %collective-permute-start.9 = (bf16[2048,128]{1,0:T(8,128)(2,1)S(1)}, bf16[2048,128]{1,0:T(8,128)(2,1)S(1)}, u32[]{:S(2)}, u32[]{:S(2)}) collective-permute-start(bf16[2048,128]{1,0:T(8,128)(2,1)S(1)} %get-tuple-element.53), channel_id=1, source_target_pairs={{0,2},{1,3},{2,0},{3,1},{4,6},{5,7},{6,4},{7,5},{8,10},{9,11},{10,... | collective-permute-start | bytes 1572872 | tf_op jit(solution)/shard_map/ppermute | solution.py:74
  24.0 14.4 %collective-permute-start.7 = (bf16[2048,128]{1,0:T(8,128)(2,1)S(1)}, bf16[2048,128]{1,0:T(8,128)(2,1)S(1)}, u32[]{:S(2)}, u32[]{:S(2)}) collective-permute-start(bf16[2048,128]{1,0:T(8,128)(2,1)S(1)} %get-tuple-element.49), channel_id=1, source_target_pairs={{0,12},{1,5},{2,50},{3,19},{4,0},{5,9},{6,54},{7,23},{8,4},{9,13},... | collective-permute-start | bytes 1572872 | tf_op jit(solution)/shard_map/ppermute | solution.py:74
  24.0 14.4 %collective-permute-start.8 = (bf16[2048,128]{1,0:T(8,128)(2,1)S(1)}, bf16[2048,128]{1,0:T(8,128)(2,1)S(1)}, u32[]{:S(2)}, u32[]{:S(2)}) collective-permute-start(bf16[2048,128]{1,0:T(8,128)(2,1)S(1)} %get-tuple-element.50), channel_id=1, source_target_pairs={{0,4},{1,13},{2,18},{3,51},{4,8},{5,1},{6,22},{7,55},{8,12},{9,5},... | collective-permute-start | bytes 1572872 | tf_op jit(solution)/shard_map/ppermute | solution.py:74
  39.2 6.5 %collective-permute-start.13 = (bf16[20,256,128]{2,1,0:T(8,128)(2,1)S(1)}, bf16[20,256,128]{2,1,0:T(8,128)(2,1)S(1)}, u32[]{:S(2)}, u32[]{:S(2)}) collective-permute-start(bf16[20,256,128]{2,1,0:T(8,128)(2,1)S(1)} %pack.5), channel_id=1, source_target_pairs={{0,1},{1,0},{2,3},{3,2},{4,5},{5,4},{6,7},{7,6},{8,9},{9,8},{10,11... | collective-permute-start | bytes 3932168 | tf_op jit(solution)/shard_map/ppermute | solution.py:74
  40.7 15.1 %collective-permute-start.12 = (bf16[2048,128]{1,0:T(8,128)(2,1)S(1)}, bf16[2048,128]{1,0:T(8,128)(2,1)S(1)}, u32[]{:S(2)}, u32[]{:S(2)}) collective-permute-start(bf16[2048,128]{1,0:T(8,128)(2,1)S(1)} %collective-permute-done.10.refs_1_), channel_id=1, source_target_pairs={{0,2},{1,3},{2,0},{3,1},{4,6},{5,7},{6,4},{7,5},{8,10},{9,11},{10,... | collective-permute-start | bytes 1572872 | tf_op jit(solution)/shard_map/ppermute | solution.py:74
  42.9 13.6 %collective-permute-start.15 = (bf16[2048,128]{1,0:T(8,128)(2,1)S(1)}, bf16[2048,128]{1,0:T(8,128)(2,1)S(1)}, u32[]{:S(2)}, u32[]{:S(2)}) collective-permute-start(bf16[2048,128]{1,0:T(8,128)(2,1)S(1)} %collective-permute-done.7.refs_4_), channel_id=1, source_target_pairs={{0,16},{1,49},{2,6},{3,15},{4,20},{5,53},{6,10},{7,3},{8,24},{9,57... | collective-permute-start | bytes 1572872 | tf_op jit(solution)/shard_map/ppermute | solution.py:74
  45.7 13.1 %collective-permute-start.16 = (bf16[2048,128]{1,0:T(8,128)(2,1)S(1)}, bf16[2048,128]{1,0:T(8,128)(2,1)S(1)}, u32[]{:S(2)}, u32[]{:S(2)}) collective-permute-start(bf16[2048,128]{1,0:T(8,128)(2,1)S(1)} %pad_maximum_fusion.4), channel_id=1, source_target_pairs={{0,48},{1,17},{2,14},{3,7},{4,52},{5,21},{6,2},{7,11},{8,56},{9,25... | collective-permute-start | bytes 1572872 | tf_op jit(solution)/shard_map/ppermute | solution.py:74
  45.7 13.1 %collective-permute-start.14 = (bf16[2048,128]{1,0:T(8,128)(2,1)S(1)}, bf16[2048,128]{1,0:T(8,128)(2,1)S(1)}, u32[]{:S(2)}, u32[]{:S(2)}) collective-permute-start(bf16[2048,128]{1,0:T(8,128)(2,1)S(1)} %collective-permute-done.10.refs_1_), channel_id=1, source_target_pairs={{0,12},{1,5},{2,50},{3,19},{4,0},{5,9},{6,54},{7,23},{8,4},{9,13},... | collective-permute-start | bytes 1572872 | tf_op jit(solution)/shard_map/ppermute | solution.py:74
  46.0 13.1 %collective-permute-start.17 = (bf16[2048,128]{1,0:T(8,128)(2,1)S(1)}, bf16[2048,128]{1,0:T(8,128)(2,1)S(1)}, u32[]{:S(2)}, u32[]{:S(2)}) collective-permute-start(bf16[2048,128]{1,0:T(8,128)(2,1)S(1)} %collective-permute-done.9.refs_2_), channel_id=1, source_target_pairs={{0,4},{1,13},{2,18},{3,51},{4,8},{5,1},{6,22},{7,55},{8,12},{9,5},... | collective-permute-start | bytes 1572872 | tf_op jit(solution)/shard_map/ppermute | solution.py:74
  59.9 5.1 %collective-permute-start.21 = (bf16[20,256,128]{2,1,0:T(8,128)(2,1)S(1)}, bf16[20,256,128]{2,1,0:T(8,128)(2,1)S(1)}, u32[]{:S(2)}, u32[]{:S(2)}) collective-permute-start(bf16[20,256,128]{2,1,0:T(8,128)(2,1)S(1)} %pack.6), channel_id=1, source_target_pairs={{0,1},{1,0},{2,3},{3,2},{4,5},{5,4},{6,7},{7,6},{8,9},{9,8},{10,11... | collective-permute-start | bytes 3932168 | tf_op jit(solution)/shard_map/ppermute | solution.py:74
  65.1 14.4 %collective-permute-start.22 = (bf16[2048,128]{1,0:T(8,128)(2,1)S(1)}, bf16[2048,128]{1,0:T(8,128)(2,1)S(1)}, u32[]{:S(2)}, u32[]{:S(2)}) collective-permute-start(bf16[2048,128]{1,0:T(8,128)(2,1)S(1)} %collective-permute-done.16.refs_1_), channel_id=1, source_target_pairs={{0,4},{1,13},{2,18},{3,51},{4,8},{5,1},{6,22},{7,55},{8,12},{9,5},... | collective-permute-start | bytes 1572872 | tf_op jit(solution)/shard_map/ppermute | solution.py:74
  67.8 10.0 %collective-permute-start.18 = (bf16[1024,128]{1,0:T(8,128)(2,1)S(1)}, bf16[1024,128]{1,0:T(8,128)(2,1)S(1)}, u32[]{:S(2)}, u32[]{:S(2)}) collective-permute-start(bf16[1024,128]{1,0:T(8,128)(2,1)S(1)} %slice.23), channel_id=1, source_target_pairs={{0,32},{1,33},{2,10},{3,11},{4,36},{5,37},{6,14},{7,15},{8,40},{9,... | collective-permute-start | bytes 786440 | tf_op jit(solution)/shard_map/ppermute | solution.py:74
  69.0 10.1 %collective-permute-start.19 = (bf16[1024,128]{1,0:T(8,128)(2,1)S(1)}, bf16[1024,128]{1,0:T(8,128)(2,1)S(1)}, u32[]{:S(2)}, u32[]{:S(2)}) collective-permute-start(bf16[1024,128]{1,0:T(8,128)(2,1)S(1)} %slice.23), channel_id=1, source_target_pairs={{0,16},{1,49},{2,6},{3,15},{4,20},{5,53},{6,10},{7,3},{8,24},{9,57... | collective-permute-start | bytes 786440 | tf_op jit(solution)/shard_map/ppermute | solution.py:74
  70.6 8.9 %collective-permute-start.20 = (bf16[1024,128]{1,0:T(8,128)(2,1)S(1)}, bf16[1024,128]{1,0:T(8,128)(2,1)S(1)}, u32[]{:S(2)}, u32[]{:S(2)}) collective-permute-start(bf16[1024,128]{1,0:T(8,128)(2,1)S(1)} %slice.24), channel_id=1, source_target_pairs={{0,2},{1,3},{2,0},{3,1},{4,6},{5,7},{6,4},{7,5},{8,10},{9,11},{10,... | collective-permute-start | bytes 786440 | tf_op jit(solution)/shard_map/ppermute | solution.py:74
  72.2 7.3 %collective-permute-start.23 = (bf16[1024,128]{1,0:T(8,128)(2,1)S(1)}, bf16[1024,128]{1,0:T(8,128)(2,1)S(1)}, u32[]{:S(2)}, u32[]{:S(2)}) collective-permute-start(bf16[1024,128]{1,0:T(8,128)(2,1)S(1)} %slice.25), channel_id=1, source_target_pairs={{0,12},{1,5},{2,50},{3,19},{4,0},{5,9},{6,54},{7,23},{8,4},{9,13},... | collective-permute-start | bytes 786440 | tf_op jit(solution)/shard_map/ppermute | solution.py:74
  80.2 2.4 %collective-permute-start.24 = (bf16[12,256,128]{2,1,0:T(8,128)(2,1)S(1)}, bf16[12,256,128]{2,1,0:T(8,128)(2,1)S(1)}, u32[]{:S(2)}, u32[]{:S(2)}) collective-permute-start(bf16[12,256,128]{2,1,0:T(8,128)(2,1)S(1)} %pack.7), channel_id=1, source_target_pairs={{0,1},{1,0},{2,3},{3,2},{4,5},{5,4},{6,7},{7,6},{8,9},{9,8},{10,11... | collective-permute-start | bytes 2359304 | tf_op jit(solution)/shard_map/ppermute | solution.py:74
  82.2 10.2 %copy-start.2 = (f32[256]{0:T(256)S(1)}, f32[256]{0:T(256)}, u32[]{:S(2)}) copy-start(f32[256]{0:T(256)} %param.11) | copy-start | bytes 3076
  84.4 8.0 %collective-permute-start.25 = (bf16[1024,128]{1,0:T(8,128)(2,1)S(1)}, bf16[1024,128]{1,0:T(8,128)(2,1)S(1)}, u32[]{:S(2)}, u32[]{:S(2)}) collective-permute-start(bf16[1024,128]{1,0:T(8,128)(2,1)S(1)} %get-tuple-element.80), channel_id=1, source_target_pairs={{0,64},{64,0},{1,65},{65,1},{2,66},{66,2},{3,67},{67,3},{4,68},{68... | collective-permute-start | bytes 786440 | tf_op jit(solution)/shard_map/ppermute | solution.py:313
